TPU v7x, 128 devices: a whole 4x4x4 slice. The times are simulated.
128 devices in a mesh: dp: 128 (over y, z, x, core).
Axes of the slice: x: 4, y: 4, z: 4, core: 2. Of those that a mesh axis runs over, the one named last changes fastest.
Arguments:
- embeddings: bfloat16 [16384, 1024], P('dp')
- positives: int32 [16384], P('dp'), may hold values from 0 to 16383, as said below
Outputs:
- loss: float32 [], replicated
- grad: float32 [16384, 1024], P('dp')
Inputs may be any that keep to these rules, and one draw needn't show every extreme that they name: positives is a perfect matching of the rows: positives[positives[i]] = i and positives[i] != i.
All inputs are finite; a program needn't handle non-finite values.
Results may differ from a plain program's by a relative error of at most 0.002.
Values may be sent and summed in bfloat16 or wider, within the bound.
A program may use at most 128 MiB of HBM per device.

v0:
```python
import math

import jax
import jax.numpy as jnp
from jax import lax
from jax.sharding import PartitionSpec as P

ITERS = 3


def sweep(scores, pull_all, cotangent, weights, before_all, before_own, lse_row, lse_col, last):
    pull = -cotangent / 2
    forward_plan = jnp.exp(scores + before_all[None, :] - lse_row[:, None])
    mirror = pull_all[None, :] * jnp.exp(scores + before_own[:, None] - lse_col[None, :])
    weights = weights + pull[:, None] * forward_plan + mirror
    if not last:
        cotangent = cotangent / 2 + jnp.sum(mirror, axis=1)
    return (cotangent, weights)


def shards(embeddings, positives):
    rows, width = embeddings.shape
    blocks = lax.axis_size("dp")
    device = lax.axis_index("dp")
    total = rows * blocks
    scale = 1.0 / math.sqrt(width)
    everyone = lax.all_gather(embeddings, "dp", axis=0, tiled=True)
    scores = jnp.dot(embeddings, everyone.T, preferred_element_type=jnp.float32) * scale
    column = jnp.arange(total, dtype=jnp.int32)
    global_row = device * rows + jnp.arange(rows, dtype=jnp.int32)
    scores = jnp.where(column[None, :] == global_row[:, None], -30000.0, scores)
    potential = jnp.zeros((rows,), jnp.float32)
    potential_all = jnp.zeros((total,), jnp.float32)
    previous_all = []
    previous_own = []
    lse_own = []
    lse_all = []
    for step in range(ITERS):
        shifted = scores + potential_all[None, :]
        top = jnp.max(shifted, axis=1)
        lse = top + jnp.log(jnp.sum(jnp.exp(shifted - top[:, None]), axis=1))
        previous_all.append(potential_all)
        previous_own.append(potential)
        lse_own.append(lse)
        potential = (potential - lse) / 2
        gathered = lax.all_gather(potential, "dp", axis=0, tiled=True)
        lse_all.append(potential_all - 2 * gathered)
        potential_all = gathered
    picked = jnp.take_along_axis(scores, positives[:, None], axis=1)[:, 0]
    local_sum = jnp.sum(picked + potential + potential_all[positives])
    cotangent = jnp.full((rows,), -2.0, jnp.float32)
    weights = -2.0 * (column[None, :] == positives[:, None]).astype(jnp.float32)
    last_step = ITERS - 1
    cotangent, weights = sweep(
        scores,
        jnp.ones((total,), jnp.float32),
        cotangent,
        weights,
        previous_all[last_step],
        previous_own[last_step],
        lse_own[last_step],
        lse_all[last_step],
        last_step == 0,
    )
    pull = -cotangent / 2
    loss = -lax.psum(local_sum, "dp") / total
    pull_all = lax.all_gather(pull, "dp", axis=0, tiled=True)
    step = ITERS - 2
    cotangent, weights = sweep(
        scores,
        pull_all,
        cotangent,
        weights,
        previous_all[step],
        previous_own[step],
        lse_own[step],
        lse_all[step],
        step == 0,
    )
    for step in reversed(range(ITERS - 2)):
        pull_all = lax.all_gather(-cotangent / 2, "dp", axis=0, tiled=True)
        cotangent, weights = sweep(
            scores,
            pull_all,
            cotangent,
            weights,
            previous_all[step],
            previous_own[step],
            lse_own[step],
            lse_all[step],
            step == 0,
        )
    grad = (
        jnp.dot(weights.astype(jnp.bfloat16), everyone, preferred_element_type=jnp.float32) * scale
    )
    return (loss, grad)


def solution(mesh):
    placed = (P("dp", None), P("dp"))
    return jax.shard_map(
        shards, mesh=mesh, in_specs=placed, out_specs=(P(), P("dp", None)), check_vma=False
    )
```

profile of v0, /device:TPU:1, one launch (start us, length us, event | category | flops | bytes accessed | tf_op | source)
XLA Modules:
  0.0 404.0 jit_solution(9886586752635744435)
XLA Ops:
  7.2 0.0 all-gather.7.cloned.1.call-start
  7.2 0.7 all-gather.7.cloned.1.call-update
  7.9 0.7 fusion.28
  8.6 112.8 %all-gather.7.cloned.1.call-done = bf16[16384,1024]{1,0:T(8,128)(2,1)} async-done(((bf16[128,1024]{1,0:T(8,128)(2,1)}), bf16[16384,1024]{1,0:T(8,128)(2,1)}) %all-gather.7.cloned.1.call-update) | async-done | bytes 33554448 | tf_op jit(solution)/shard_map/all_gather | solution.py:27
  121.4 19.3 %fusion.29 = (f32[128]{0:T(128)S(1)}, f32[128,16384]{1,0:T(8,128)}) fusion(bf16[128,1024]{1,0:T(8,128)(2,1)} %param.2, bf16[16384,1024]{1,0:T(8,128)(2,1)} %all-gather.7.cloned.1.call-done, s32[128]{0:T(128)S(1)} %iota_add_fusion), kind=kOutput, calls=%fused_computation.60 | convolution fusion | flops 4303355904 | bytes 42206208 | tf_op jit(solution)/shard_map/dot_general | solution.py:28
  140.7 2.0 gather_fusion.1
  142.7 0.0 copy-start
  142.7 4.8 %exponential_reduce_fusion.2 = f32[128]{0:T(128)S(1)} fusion(f32[128,16384]{1,0:T(8,128)} %get-tuple-element.16, f32[128]{0:T(128)S(1)} %get-tuple-element.15), kind=kLoop, calls=%fused_computation.12 | loop fusion | flops 4194176 | bytes 8389632 | tf_op jit(solution)/shard_map/reduce_sum | solution.py:41
  147.6 30.9 %all-gather = f32[128,1,128]{2,1,0:T(1,128)S(1)} all-gather(f32[1,1,128]{2,1,0:T(1,128)S(1)} %fusion.27), channel_id=1, replica_groups=mesh['dp'=128] {'dp'}, dimensions={0}, use_global_device_ids=true | all-gather | bytes 66048 | tf_op jit(solution)/shard_map/all_gather | solution.py:46
  178.4 0.0 copy-done
  178.4 0.7 add_reduce_fusion.1
  179.1 1.8 exponential_reduce_fusion.1
  180.9 29.6 %all-gather.1 = f32[128,1,128]{2,1,0:T(1,128)S(1)} all-gather(f32[1,1,128]{2,1,0:T(1,128)S(1)} %bitcast.35), channel_id=1, replica_groups=mesh['dp'=128] {'dp'}, dimensions={0}, use_global_device_ids=true | all-gather | bytes 66048 | tf_op jit(solution)/shard_map/all_gather | solution.py:46
  210.5 0.0 copy-start.1
  210.5 0.7 add_reduce_fusion
  211.1 1.8 exponential_reduce_fusion
  212.9 29.7 %all-gather.2 = f32[128,1,128]{2,1,0:T(1,128)S(1)} all-gather(f32[1,1,128]{2,1,0:T(1,128)S(1)} %get-tuple-element.4), channel_id=1, replica_groups=mesh['dp'=128] {'dp'}, dimensions={0}, use_global_device_ids=true | all-gather | bytes 66048 | tf_op jit(solution)/shard_map/all_gather | solution.py:46
  242.6 1.1 gather_fusion
  243.8 0.0 copy-done.1
  243.8 0.6 add_reduce_fusion.2
  244.4 62.6 %psum.7 = f32[]{:T(128)} all-reduce(f32[]{:T(128)} %add_reduce_fusion.2), channel_id=1, replica_groups=mesh['dp'=128] {'dp'}, use_global_device_ids=true, to_apply=%region_7.8 | all-reduce | flops 1 | bytes 8 | tf_op jit(solution)/shard_map/psum | solution.py:66
  307.6 4.9 %fusion.2 = f32[128]{0:T(128)S(1)} fusion(f32[128,16384]{1,0:T(8,128)} %get-tuple-element.16, f32[16384]{0:T(1024)S(1)} %get-tuple-element.8, f32[128]{0:T(128)S(1)} %get-tuple-element.6), kind=kLoop, calls=%fused_computation.8 | loop fusion | flops 6291328 | bytes 8455168 | tf_op jit(solution)/shard_map/reduce_sum | solution.py:17
  312.5 29.6 %all-gather.3 = f32[128,1,128]{2,1,0:T(1,128)S(1)} all-gather(f32[1,1,128]{2,1,0:T(1,128)S(1)} %get-tuple-element.12), channel_id=1, replica_groups=mesh['dp'=128] {'dp'}, dimensions={0}, use_global_device_ids=true | all-gather | bytes 66048 | tf_op jit(solution)/shard_map/all_gather | solution.py:67
  342.2 5.2 %fusion.1 = f32[128]{0:T(128)S(1)} fusion(f32[128,16384]{1,0:T(8,128)} %get-tuple-element.16, f32[16384]{0:T(1024)S(1)} %get-tuple-element.9, f32[128]{0:T(128)S(1)} %get-tuple-element.2, f32[16384]{0:T(1024)S(1)} %bitcast.32), kind=kLoop, calls=%fused_computation.6 | loop fusion | flops 8388480 | bytes 8520704 | tf_op jit(solution)/shard_map/reduce_sum | solution.py:17
  347.4 29.0 %all-gather.4 = f32[128,1,128]{2,1,0:T(1,128)S(1)} all-gather(f32[1,1,128]{2,1,0:T(1,128)S(1)} %bitcast.36), channel_id=1, replica_groups=mesh['dp'=128] {'dp'}, dimensions={0}, use_global_device_ids=true | all-gather | bytes 66048 | tf_op jit(solution)/shard_map/all_gather | solution.py:81
  376.3 19.7 %fusion.21 = f32[128,1024]{1,0:T(8,128)} fusion(bf16[16384,1024]{1,0:T(8,128)(2,1)} %all-gather.7.cloned.1.call-done, f32[128,16384]{1,0:T(8,128)} %get-tuple-element.16, f32[16384]{0:T(1024)S(1)} %get-tuple-element.10, f32[16384]{0:T(1024)S(1)} %bitcast.34, f32[128]{0:T(128)S(1)} %get-tuple-element.3, f32[128]{0:T(128)S(1)} %negate_multiply_fusion, ...), kind=kOutput, calls=%fused_computation.34 | convolution fusion | flops 4343332864 | bytes 42930176 | tf_op jit(solution)/shard_map/dot_general | solution.py:94
  (12 shorter events, 0.1 us)
Async XLA Ops:
  7.2 114.2 %all-gather.7.cloned.1.call-start = ((), (), s32[]{:S(2)}) async-start(), calls=%async_computation | async-start | bytes 33816576 | tf_op jit(solution)/shard_map/all_gather | solution.py:27
  142.7 35.7 %copy-start = (f32[128,16384]{1,0:T(8,128)S(1)}, f32[128,16384]{1,0:T(8,128)}, u32[]{:S(2)}) copy-start(f32[128,16384]{1,0:T(8,128)} %get-tuple-element.16) | copy-start | bytes 25165828
  210.5 33.3 %copy-start.1 = (s32[128]{0:T(128)S(1)}, s32[128]{0:T(128)}, u32[]{:S(2)}) copy-start(s32[128]{0:T(128)} %param.3) | copy-start | bytes 1540
Sparse Core Ops, SparseCore 0:
  11.0 110.3 all-gather.6
where the time goes:
time: 404 us
  blocking collectives  211 us (52%)
  waiting for transfers between devices  113 us (28%)
  matrix products  39 us (10%)
  other arithmetic  21.1 us (5%)
  between operations  15.9 us (4%)
    all_gather x1, waiting for transfers between devices, shards(): everyone = lax.all_gather(embeddings, 'dp', axis=0, tiled=True)  113 us
    all_gather x3, blocking collectives, shards(): gathered = lax.all_gather(potential, 'dp', axis=0, tiled=True)  90.1 us
    psum x1, blocking collectives, shards(): loss = -lax.psum(local_sum, 'dp') / total  62.6 us
    all_gather x1, blocking collectives, shards(): pull_all = lax.all_gather(pull, 'dp', axis=0, tiled=True)  29.6 us
    all_gather x1, blocking collectives, shards(): pull_all = lax.all_gather(-cotangent / 2, 'dp', axis=0, tiled=True)  29 us
    dot_general x1, matrix products, shards(): jnp.dot(weights.astype(jnp.bfloat16), everyone, preferred_element_type=jn...  19.7 us
    dot_general x1, matrix products, shards(): jnp.dot(embeddings, everyone.T, preferred_element_type=jnp.float32) * scale  19.3 us
    reduce_sum x2, other arithmetic, sweep(): cotangent = cotangent / 2 + jnp.sum(mirror, axis=1)  10.1 us
  transfers between devices with their start and end apart: 1, of which 1 were waited for; matrix products, arithmetic and copies ran while one was open for 0% of the time, Pallas kernels for 0%

commit v1 on v0

v1 whole, which is shorter than its diff:
```python
import functools
import math

import jax
import jax.numpy as jnp
from jax import lax
from jax.experimental import pallas as pl
from jax.experimental.pallas import tpu as pltpu
from jax.sharding import PartitionSpec as P

SIDE = 4
PLANE = SIDE * SIDE
LINE = SIDE * 2
BLOCK = 128
WIDTH = 1024
RROWS = LINE * BLOCK
CCOLS = PLANE * BLOCK
TOTAL = PLANE * RROWS
LOG2E = math.log2(math.e)
LN2 = math.log(2.0)
MESH = pl.DeviceIdType.MESH
F32 = jnp.float32
BF16 = jnp.bfloat16
CH = 32
OFFS = (0, -1, 1, 2)


def fold(v, op):
    out = v[0:8]
    for r in range(8, v.shape[0], 8):
        out = op(out, v[r : r + 8])
    return out


def log2(v):
    return jnp.log(v) * LOG2E


def kernel(
    emb, pos, grad, loss,
    ec, er, s, w, wb, rvec, cvec, pr_ref, mr, accr, cmsg, crx, rmsg, rrx,
    gp, rb, xs2, xr2, xs1, xr1,
    lsem, psend, prsem, xsend, xrsem, csend, crecv, rsend, rrecv, gsend, grecv, hsend, hrecv,
):
    me = lax.axis_index("dp")
    a = me // LINE
    b = me % LINE
    y, z = a // SIDE, a % SIDE
    x, core = b // 2, b % 2

    def in_plane(k):
        return lax.rem(a + k, PLANE) * LINE + b

    def in_line(k):
        return a * LINE + lax.rem(b + k, LINE)

    barrier = pltpu.get_barrier_semaphore()

    def greet_plane(k, carry):
        pl.semaphore_signal(barrier, inc=1, device_id=(in_plane(k),), device_id_type=MESH)
        return carry

    def greet_line(k, carry):
        pl.semaphore_signal(barrier, inc=1, device_id=(in_line(k),), device_id_type=MESH)
        return carry

    lax.fori_loop(1, PLANE, greet_plane, 0)
    lax.fori_loop(1, LINE, greet_line, 0)
    own_c = pltpu.make_async_copy(emb, ec.at[a], lsem.at[0])
    own_r = pltpu.make_async_copy(emb, er.at[b], lsem.at[1])
    own_c.start()
    own_r.start()
    pl.semaphore_wait(barrier, PLANE - 1 + LINE - 1)

    def blk(h, op, oq):
        dy, dz = (oq, op) if h == 0 else (op, oq)
        return lax.rem(y + dy + SIDE, SIDE) * SIDE + lax.rem(z + dz + SIDE, SIDE)

    def send_plane(h, op, oq, lo, n, tp, tq, idx):
        k = blk(h, op, oq)
        rows = pl.ds(64 * h + lo, n)
        src = emb.at[rows] if (op, oq) == (0, 0) else ec.at[k, rows]
        pltpu.make_async_remote_copy(
            src_ref=src, dst_ref=ec.at[k, rows], send_sem=psend, recv_sem=prsem.at[h, idx],
            device_id=(blk(h, tp, tq) * LINE + b,), device_id_type=MESH,
        ).start()

    def wait_plane(h, op, oq, lo, n, idx):
        ref = ec.at[blk(h, op, oq), pl.ds(64 * h + lo, n)]
        pltpu.make_async_copy(ref, ref, prsem.at[h, idx]).wait()

    def xdev(dx):
        return a * LINE + lax.rem(x + dx + SIDE, SIDE) * 2 + core

    sibling = a * LINE + x * 2 + (1 - core)

    def xblk(dx):
        return lax.rem(x + dx + SIDE, SIDE) * 2 + core

    def send_line(dx, lo, n, device, idx):
        k = xblk(dx)
        rows = pl.ds(lo, n)
        src = emb.at[rows] if dx == 0 else er.at[k, rows]
        pltpu.make_async_remote_copy(
            src_ref=src, dst_ref=er.at[k, rows], send_sem=xsend, recv_sem=xrsem.at[idx],
            device_id=(device,), device_id_type=MESH,
        ).start()

    def wait_line(k, lo, n, idx):
        ref = er.at[k, pl.ds(lo, n)]
        pltpu.make_async_copy(ref, ref, xrsem.at[idx]).wait()

    for h in (0, 1):
        send_plane(h, 0, 0, 0, 64, 1, 0, 0)
        send_plane(h, 0, 0, 0, 64, -1, 0, 1)
    send_line(0, 0, 128, xdev(1), 0)
    send_line(0, 0, 128, xdev(-1), 1)
    send_line(0, 0, 128, sibling, 4)
    for h in (0, 1):
        send_plane(h, 0, 0, 0, 64, 0, 1, 4)
        send_plane(h, 0, 0, 0, 64, 0, -1, 5)
    for h in (0, 1):
        wait_plane(h, -1, 0, 0, 64, 0)
        send_plane(h, -1, 0, 0, 32, 1, 0, 2)
        wait_plane(h, 1, 0, 0, 64, 1)
        send_plane(h, 1, 0, 32, 32, -1, 0, 3)
    wait_line(xblk(-1), 0, 128, 0)
    send_line(-1, 0, 64, xdev(1), 2)
    send_line(-1, 0, 128, sibling, 5)
    wait_line(xblk(1), 0, 128, 1)
    send_line(1, 64, 64, xdev(-1), 3)
    send_line(1, 0, 128, sibling, 6)
    for h in (0, 1):
        for oi in (1, 2):
            send_plane(h, OFFS[oi], 0, 0, 64, 0, 1, 4 + 4 * oi)
            send_plane(h, OFFS[oi], 0, 0, 64, 0, -1, 5 + 4 * oi)
    for h in (0, 1):
        wait_plane(h, 0, -1, 0, 64, 4)
        send_plane(h, 0, -1, 0, 32, 0, 1, 6)
        wait_plane(h, 0, 1, 0, 64, 5)
        send_plane(h, 0, 1, 32, 32, 0, -1, 7)
    for h in (0, 1):
        wait_plane(h, 2, 0, 0, 32, 2)
        wait_plane(h, 2, 0, 32, 32, 3)
        send_plane(h, 2, 0, 0, 64, 0, 1, 16)
        send_plane(h, 2, 0, 0, 64, 0, -1, 17)
    wait_line(xblk(2), 0, 64, 2)
    wait_line(xblk(2), 64, 64, 3)
    send_line(2, 0, 128, sibling, 7)
    for oi in (1, 2, 3):
        o = OFFS[oi]
        for h in (0, 1):
            wait_plane(h, o, -1, 0, 64, 4 + 4 * oi)
            send_plane(h, o, -1, 0, 32, 0, 1, 6 + 4 * oi)
            wait_plane(h, o, 1, 0, 64, 5 + 4 * oi)
            send_plane(h, o, 1, 32, 32, 0, -1, 7 + 4 * oi)
    for i, dx in enumerate((0, -1, 1, 2)):
        wait_line(lax.rem(x + dx + SIDE, SIDE) * 2 + (1 - core), 0, 128, 4 + i)
    for oi in range(4):
        for h in (0, 1):
            wait_plane(h, OFFS[oi], 2, 0, 32, 6 + 4 * oi)
            wait_plane(h, OFFS[oi], 2, 32, 32, 7 + 4 * oi)
    own_c.wait()
    own_r.wait()

    score_scale = LOG2E / math.sqrt(WIDTH)

    def score_tile(t, carry):
        n, m = t // 4, t % 4
        left = er[pl.ds(2 * m, 2)].reshape(2 * BLOCK, WIDTH)
        right = ec[pl.ds(2 * n, 2)].reshape(2 * BLOCK, WIDTH)
        out = lax.dot_general(left, right, (((1,), (1,)), ((), ())), preferred_element_type=F32)
        s[pl.ds(pl.multiple_of(m * 256, 256), 256), pl.ds(pl.multiple_of(n * 256, 256), 256)] = out * score_scale
        return carry

    lax.fori_loop(0, 32, score_tile, 0)
    eye = lax.broadcasted_iota(jnp.int32, (BLOCK, BLOCK), 0) == lax.broadcasted_iota(jnp.int32, (BLOCK, BLOCK), 1)
    dr = pl.ds(pl.multiple_of(b * BLOCK, BLOCK), BLOCK)
    dc = pl.ds(pl.multiple_of(a * BLOCK, BLOCK), BLOCK)
    s[dr, dc] = jnp.where(eye, -30000.0 * LOG2E, s[dr, dc])

    def rows_at(i):
        return pl.ds(pl.multiple_of(i * CH, CH), CH)

    def lanes(k):
        return slice(k * BLOCK, (k + 1) * BLOCK)

    def to_rows(v, ref):
        for g in range(LINE):
            ref[pl.ds(g * BLOCK, BLOCK), :] = jnp.broadcast_to(v[g : g + 1], (BLOCK, BLOCK)).T

    def from_rows(ref):
        out = []
        for g in range(LINE):
            v = jnp.where(eye, ref[pl.ds(g * BLOCK, BLOCK), :], 0.0)
            out.append(jnp.sum(v, axis=0, keepdims=True))
        return jnp.concatenate(out, axis=0)

    def exchange(e):
        def to_plane(k, carry):
            pltpu.make_async_remote_copy(
                src_ref=cmsg.at[e], dst_ref=crx.at[e, a], send_sem=csend.at[e], recv_sem=crecv.at[e],
                device_id=(in_plane(k),), device_id_type=MESH,
            ).start()
            return carry

        def to_line(k, carry):
            pltpu.make_async_remote_copy(
                src_ref=rmsg.at[e], dst_ref=rrx.at[e, b], send_sem=rsend.at[e], recv_sem=rrecv.at[e],
                device_id=(in_line(k),), device_id_type=MESH,
            ).start()
            return carry

        lax.fori_loop(1, LINE, to_line, 0)
        lax.fori_loop(1, PLANE, to_plane, 0)
        crx[e, a] = cmsg[e]
        rrx[e, b] = rmsg[e]
        call = crx.at[e, pl.ds(0, PLANE - 1)]
        rall = rrx.at[e, pl.ds(0, LINE - 1)]
        pltpu.make_async_copy(rall, rall, rrecv.at[e]).wait()
        pltpu.make_async_copy(call, call, crecv.at[e]).wait()
        pltpu.make_async_copy(rall, rall, rsend.at[e]).wait()
        pltpu.make_async_copy(call, call, csend.at[e]).wait()

    def merge(v):
        top = jnp.max(v, axis=0)
        return top + log2(jnp.sum(jnp.exp2(v - top[None]), axis=0))

    def forward(t):
        pot_r, pot_c = rvec.at[t - 2], cvec.at[t - 2]

        def top_step(i, tops):
            rows = rows_at(i)
            if t > 1:
                pr = pot_r[rows, :]
            best = None
            out = []
            for k in range(PLANE):
                v = s[rows, lanes(k)]
                u = v + pot_c[k : k + 1, :] if t > 1 else v
                q = v + pr if t > 1 else v
                best = u if best is None else jnp.maximum(best, u)
                out.append(jnp.maximum(tops[k], fold(q, jnp.maximum)))
            mr[rows, :] = jnp.broadcast_to(jnp.max(best, axis=1, keepdims=True), (CH, BLOCK))
            return tuple(out)

        low = jnp.full((8, BLOCK), -jnp.inf, F32)
        tops = lax.fori_loop(0, RROWS // CH, top_step, (low,) * PLANE)
        ctop = jnp.concatenate([jnp.max(v, axis=0, keepdims=True) for v in tops], axis=0)
        cvec[7] = ctop

        def sum_step(i, sums):
            rows = rows_at(i)
            m = mr[rows, :]
            if t > 1:
                pr = pot_r[rows, :]
            acc = None
            out = []
            for k in range(PLANE):
                v = s[rows, lanes(k)]
                u = v + pot_c[k : k + 1, :] if t > 1 else v
                q = v + pr if t > 1 else v
                p = jnp.exp2(u - m)
                acc = p if acc is None else acc + p
                out.append(sums[k] + fold(jnp.exp2(q - cvec[7, k : k + 1, :]), jnp.add))
            total = jnp.sum(acc, axis=1, keepdims=True)
            accr[rows, :] = m + log2(jnp.broadcast_to(total, (CH, BLOCK)))
            return tuple(out)

        zero = jnp.zeros((8, BLOCK), F32)
        sums = lax.fori_loop(0, RROWS // CH, sum_step, (zero,) * PLANE)
        csum = jnp.concatenate([jnp.sum(v, axis=0, keepdims=True) for v in sums], axis=0)
        cmsg[t - 1, 0:PLANE, :] = ctop + log2(csum)
        rmsg[t - 1, 0:LINE, :] = from_rows(accr)
        if t == 1:
            rmsg[0, LINE : LINE + 8, :] = jnp.broadcast_to(pos[...].astype(F32), (8, BLOCK))
        exchange(t - 1)
        lse_c = merge(crx[t - 1, :, 0:PLANE, :])
        lse_r = merge(rrx[t - 1, :, 0:LINE, :])
        return lse_r, lse_c

    cmsg[...] = jnp.zeros_like(cmsg)
    rmsg[...] = jnp.zeros_like(rmsg)
    pot_r = jnp.zeros((LINE, BLOCK), F32)
    pot_c = jnp.zeros((PLANE, BLOCK), F32)
    for t in (1, 2, 3):
        lse_r, lse_c = forward(t)
        pot_r = (pot_r - lse_r) * 0.5
        pot_c = (pot_c - lse_c) * 0.5
        to_rows(lse_r, rvec.at[t + 1])
        cvec[t + 1] = lse_c
        if t < 3:
            to_rows(pot_r, rvec.at[t - 1])
            cvec[t - 1] = pot_c
        if t == 1:
            to_rows(jnp.concatenate([rrx[0, g, LINE : LINE + 1, :] for g in range(LINE)], axis=0), pr_ref)

    first_col = (lax.broadcasted_iota(jnp.int32, (8, BLOCK), 1) + b * BLOCK).astype(F32)
    first_col = jnp.broadcast_to(first_col[0:1], (CH, BLOCK))

    def backward(t):
        pot_rr, pot_cc = rvec.at[t - 2], cvec.at[t - 2]
        lse_rr, lse_cc = rvec.at[t + 1], cvec.at[t + 1]
        pull_rr, pull_cc = rvec.at[7 - t], cvec.at[7 - t]

        def step(i, carry):
            sums, picked = carry
            rows = rows_at(i)
            lr = lse_rr[rows, :]
            if t > 1:
                pr = pot_rr[rows, :]
            if t < 3:
                qr = pull_rr[rows, :]
            else:
                partner = pr_ref[rows, :] - first_col
            acc = None
            out = []
            for k in range(PLANE):
                v = s[rows, lanes(k)]
                u = v + pot_cc[k : k + 1, :] if t > 1 else v
                q = v + pr if t > 1 else v
                term = jnp.exp2(u - lr)
                mirror = jnp.exp2(q - lse_cc[k : k + 1, :])
                if t < 3:
                    term = term * qr
                    mirror = mirror * pull_cc[k : k + 1, :]
                    total = w[rows, lanes(k)] + (term + mirror)
                else:
                    hit = partner == float(k * RROWS)
                    picked = picked + fold(jnp.where(hit, v, 0.0), jnp.add)
                    total = jnp.where(hit, -2.0, 0.0) + (term + mirror)
                if t > 1:
                    w[rows, lanes(k)] = total
                    out.append(sums[k] + fold(term, jnp.add))
                    acc = mirror if acc is None else acc + mirror
                else:
                    wb[rows, lanes(k)] = total.astype(BF16)
            if t > 1:
                accr[rows, :] = jnp.broadcast_to(jnp.sum(acc, axis=1, keepdims=True), (CH, BLOCK))
            return tuple(out), picked

        zero = jnp.zeros((8, BLOCK), F32)
        sums, picked = lax.fori_loop(0, RROWS // CH, step, ((zero,) * (PLANE if t > 1 else 0), zero))
        if t == 1:
            return None
        e = 6 - t
        cmsg[e, 0:PLANE, :] = jnp.concatenate([jnp.sum(v, axis=0, keepdims=True) for v in sums], axis=0)
        rmsg[e, 0:LINE, :] = from_rows(accr)
        if t == 3:
            cmsg[e, PLANE : PLANE + 8, :] = picked
        return e

    e = backward(3)
    exchange(e)
    cot_r = -1.0 + jnp.sum(rrx[e, :, 0:LINE, :], axis=0)
    cot_c = -1.0 + jnp.sum(crx[e, :, 0:PLANE, :], axis=0)
    picked = jnp.sum(crx[e, :, PLANE : PLANE + 8, :], axis=0)
    to_rows(-0.5 * cot_r, rvec.at[5])
    cvec[5] = -0.5 * cot_c
    e = backward(2)
    rmsg[e, LINE : LINE + 8, :] = picked + 2.0 * (pot_c[0:8] + pot_c[8:16])
    exchange(e)
    cot_r = 0.5 * cot_r + jnp.sum(rrx[e, :, 0:LINE, :], axis=0)
    cot_c = 0.5 * cot_c + jnp.sum(crx[e, :, 0:PLANE, :], axis=0)
    whole = jnp.sum(rrx[e, :, LINE : LINE + 8, :], axis=0)
    loss[0, 0] = jnp.sum(whole) * (-LN2 / TOTAL)
    to_rows(-0.5 * cot_r, rvec.at[6])
    cvec[6] = -0.5 * cot_c
    backward(1)

    grad_scale = 1.0 / math.sqrt(WIDTH)

    def partial(d):
        xx = lax.rem(x + d, SIDE)
        rows = pl.ds(pl.multiple_of(xx * 256, 256), 256)

        def tile(n, carry):
            cols = pl.ds(pl.multiple_of(n * 256, 256), 256)
            right = ec[:, :, cols].reshape(CCOLS, 256)
            out = jnp.dot(wb[rows, :], right, preferred_element_type=F32) * grad_scale
            gp[d, :, :, cols] = out.reshape(2, BLOCK, 256)
            return carry

        lax.fori_loop(0, WIDTH // 256, tile, 0)
        pltpu.make_async_remote_copy(
            src_ref=gp.at[d, 1 - core], dst_ref=rb.at[d], send_sem=gsend.at[d], recv_sem=grecv.at[d],
            device_id=(sibling,), device_id_type=MESH,
        ).start()

    def chip_sum(d):
        pltpu.make_async_copy(rb.at[d], rb.at[d], grecv.at[d]).wait()
        return gp[d, core] + rb[d]

    def ring(src, dst, i, device):
        return pltpu.make_async_remote_copy(
            src_ref=src, dst_ref=dst, send_sem=hsend.at[i], recv_sem=hrecv.at[i],
            device_id=(device,), device_id_type=MESH,
        )

    half = WIDTH // 2
    far = [ring(xs2.at[i], xr2.at[i], i, xdev(dx)) for i, dx in ((0, 1), (1, -1))]
    near = [ring(xs1.at[i], xr1.at[i], 2 + i, xdev(dx)) for i, dx in ((0, 1), (1, -1))]
    partial(2)
    partial(1)
    v = chip_sum(2).astype(BF16)
    xs2[0] = v[:, :half]
    xs2[1] = v[:, half:]
    far[0].start()
    far[1].start()
    partial(3)
    v = chip_sum(1)
    far[0].wait_recv()
    xs1[0, :, :half] = (v[:, :half] + xr2[0].astype(F32)).astype(BF16)
    xs1[0, :, half:] = v[:, half:].astype(BF16)
    near[0].start()
    partial(0)
    v = chip_sum(3)
    far[1].wait_recv()
    xs1[1, :, :half] = v[:, :half].astype(BF16)
    xs1[1, :, half:] = (v[:, half:] + xr2[1].astype(F32)).astype(BF16)
    near[1].start()
    v = chip_sum(0)
    near[0].wait_recv()
    v = v + xr1[0].astype(F32)
    near[1].wait_recv()
    grad[...] = v + xr1[1].astype(F32)

    sent = ec.at[pl.ds(0, PLANE - 1)]
    pltpu.make_async_copy(sent, sent, psend).wait()
    sent = er.at[pl.ds(0, LINE - 1)]
    pltpu.make_async_copy(sent, sent, xsend).wait()
    for d in range(SIDE):
        pltpu.make_async_copy(rb.at[d], rb.at[d], gsend.at[d]).wait()
    for c in far + near:
        c.wait_send()


def shards(embeddings, positives):
    vec = pltpu.VMEM
    dma = pltpu.SemaphoreType.DMA
    grad, loss = pl.pallas_call(
        kernel,
        out_shape=(
            jax.ShapeDtypeStruct((BLOCK, WIDTH), F32),
            jax.ShapeDtypeStruct((1, 1), F32),
        ),
        in_specs=[pl.BlockSpec(memory_space=pl.ANY), pl.BlockSpec(memory_space=pltpu.VMEM)],
        out_specs=(pl.BlockSpec(memory_space=pltpu.VMEM), pl.BlockSpec(memory_space=pltpu.SMEM)),
        scratch_shapes=[
            vec((PLANE, BLOCK, WIDTH), BF16),
            vec((LINE, BLOCK, WIDTH), BF16),
            vec((RROWS, CCOLS), F32),
            vec((RROWS, CCOLS), F32),
            vec((RROWS, CCOLS), BF16),
            vec((7, RROWS, BLOCK), F32),
            vec((8, PLANE, BLOCK), F32),
            vec((RROWS, BLOCK), F32),
            vec((RROWS, BLOCK), F32),
            vec((RROWS, BLOCK), F32),
            vec((5, PLANE + 8, BLOCK), F32),
            vec((5, PLANE, PLANE + 8, BLOCK), F32),
            vec((5, LINE + 8, BLOCK), F32),
            vec((5, LINE, LINE + 8, BLOCK), F32),
            vec((SIDE, 2, BLOCK, WIDTH), F32),
            vec((SIDE, BLOCK, WIDTH), F32),
            vec((2, BLOCK, WIDTH // 2), BF16),
            vec((2, BLOCK, WIDTH // 2), BF16),
            vec((2, BLOCK, WIDTH), BF16),
            vec((2, BLOCK, WIDTH), BF16),
            dma((2,)),
            dma,
            dma((2, 20)),
            dma,
            dma((8,)),
            dma((5,)),
            dma((5,)),
            dma((5,)),
            dma((5,)),
            dma((SIDE,)),
            dma((SIDE,)),
            dma((4,)),
            dma((4,)),
        ],
        compiler_params=pltpu.CompilerParams(
            collective_id=0, has_side_effects=True, vmem_limit_bytes=56 * 1024 * 1024
        ),
    )(embeddings, positives.reshape(1, BLOCK))
    return loss.reshape(()), grad


def solution(mesh):
    placed = (P("dp", None), P("dp"))
    return jax.shard_map(
        shards, mesh=mesh, in_specs=placed, out_specs=(P(), P("dp", None)), check_vma=False
    )
```

time: 404 us -> 133 us (0.33)
  blocking collectives: 211 us -> 0 us
  Pallas kernels: 0 us -> 128 us
  waiting for transfers between devices: 113 us -> 0 us
  matrix products: 39 us -> 0 us
  other arithmetic: 21.1 us -> 0 us
  between operations: 15.9 us -> 2.33 us
    all_gather x5 -> x0, blocking collectives: 149 us -> none  [the longest x3 90.1 us: shards(): gathered = lax.all_gather(potential, 'dp', axis=0, tiled=True)]
    pallas_call x0 -> x1, Pallas kernels: none -> 128 us  [shards(): pl.pallas_call(kernel, out_shape=(jax.ShapeDtypeStruct((BLOCK, WIDTH), F3...]
    all_gather x1 -> x0, waiting for transfers between devices: 113 us -> none  [shards(): everyone = lax.all_gather(embeddings, 'dp', axis=0, tiled=True)]
    psum x1 -> x0, blocking collectives: 62.6 us -> none  [shards(): loss = -lax.psum(local_sum, 'dp') / total]
    dot_general x2 -> x0, matrix products: 39 us -> none  [the longest x1 19.7 us: shards(): jnp.dot(weights.astype(jnp.bfloat16), everyone, preferred_element_type=jn...]
    reduce_sum x6 -> x0, other arithmetic: 19 us -> none  [the longest x2 10.1 us: sweep(): cotangent = cotangent / 2 + jnp.sum(mirror, axis=1)]
  transfers between devices with their start and end apart: 1 -> 0, of which waited for: 1 -> 0; matrix products, arithmetic and copies ran while one was open for 0% -> 0% of each run, Pallas kernels for 0% -> 0%
where the time goes in v1:
time: 133 us; the launch traced here: 132 us
  Pallas kernels  128 us (96%)
  between operations  2.33 us (2%)
  local copies, waits for them, and re-layouts  1.89 us (1%)
    pallas_call x1, Pallas kernels, shards(): pl.pallas_call(kernel, out_shape=(jax.ShapeDtypeStruct((BLOCK, WIDTH), F3...  128 us

profile of v1, /device:TPU:1, one launch (start us, length us, event | category | flops | bytes accessed | tf_op | source)
XLA Modules:
  0.0 132.2 jit_solution(10429895675228284028)
XLA Ops:
  0.6 128.0 %shard_map.41 = (f32[128,1024]{1,0:T(8,128)}, f32[1,1]{1,0:T(1,128)}) custom-call(bf16[128,1024]{1,0:T(8,128)(2,1)} %emb.1, s32[1,128]{1,0:T(1,128)} %bitcast.2), custom_call_target="tpu_custom_call" | custom-call | tf_op jit(solution)/shard_map/pallas_call | solution.py:441
  129.2 1.9 %copy.7 = f32[128,1024]{1,0:T(8,128)} copy(f32[128,1024]{1,0:T(8,128)} %get-tuple-element.9) | data formatting | bytes 1048576

commit v2 on v1

--- a/solution.py
+++ b/solution.py
@@ -21,6 +21,7 @@
 MESH = pl.DeviceIdType.MESH
 F32 = jnp.float32
 BF16 = jnp.bfloat16
+SCORE_M = 4
 CH = 32
 OFFS = (0, -1, 1, 2)
 
@@ -54,23 +55,23 @@
     def in_line(k):
         return a * LINE + lax.rem(b + k, LINE)
 
+    def dev_of(dy, dz, dx, c):
+        yy, zz, xx = (lax.rem(v + d + SIDE, SIDE) for v, d in ((y, dy), (z, dz), (x, dx)))
+        return ((yy * SIDE + zz) * SIDE + xx) * 2 + c
+
     barrier = pltpu.get_barrier_semaphore()
 
-    def greet_plane(k, carry):
-        pl.semaphore_signal(barrier, inc=1, device_id=(in_plane(k),), device_id_type=MESH)
-        return carry
-
-    def greet_line(k, carry):
-        pl.semaphore_signal(barrier, inc=1, device_id=(in_line(k),), device_id_type=MESH)
-        return carry
-
-    lax.fori_loop(1, PLANE, greet_plane, 0)
-    lax.fori_loop(1, LINE, greet_line, 0)
+    near_by = (
+        [dev_of(dy, dz, dx, core) for dy, dz, dx in ((1, 0, 0), (-1, 0, 0), (0, 1, 0), (0, -1, 0), (0, 0, 1), (0, 0, -1))]
+        + [dev_of(0, 0, 0, 1 - core)]
+    )
+    for device in near_by:
+        pl.semaphore_signal(barrier, inc=1, device_id=(device,), device_id_type=MESH)
     own_c = pltpu.make_async_copy(emb, ec.at[a], lsem.at[0])
     own_r = pltpu.make_async_copy(emb, er.at[b], lsem.at[1])
     own_c.start()
     own_r.start()
-    pl.semaphore_wait(barrier, PLANE - 1 + LINE - 1)
+    pl.semaphore_wait(barrier, len(near_by))
 
     def blk(h, op, oq):
         dy, dz = (oq, op) if h == 0 else (op, oq)
@@ -147,33 +148,58 @@
     wait_line(xblk(2), 0, 64, 2)
     wait_line(xblk(2), 64, 64, 3)
     send_line(2, 0, 128, sibling, 7)
-    for oi in (1, 2, 3):
+    for i, dx in enumerate((0, -1, 1, 2)):
+        wait_line(lax.rem(x + dx + SIDE, SIDE) * 2 + (1 - core), 0, 128, 4 + i)
+    own_c.wait()
+    own_r.wait()
+
+    score_scale = LOG2E / math.sqrt(WIDTH)
+
+    def score_tile(dy, other):
+        half = z // 2
+        n = lax.rem(y + dy + SIDE, SIDE) * 2 + (1 - half if other else half)
+        right = ec[pl.ds(2 * n, 2)].reshape(2 * BLOCK, WIDTH)
+        cols = pl.ds(pl.multiple_of(n * 256, 256), 256)
+
+        def part(m, carry):
+            left = er[pl.ds(SCORE_M * m, SCORE_M)].reshape(SCORE_M * BLOCK, WIDTH)
+            out = lax.dot_general(left, right, (((1,), (1,)), ((), ())), preferred_element_type=F32)
+            s[pl.ds(pl.multiple_of(m * (SCORE_M * BLOCK), SCORE_M * BLOCK), SCORE_M * BLOCK), cols] = out * score_scale
+            return carry
+
+        lax.fori_loop(0, LINE // SCORE_M, part, 0)
+
+    def wait_forwarded(h, oi):
+        wait_plane(h, OFFS[oi], 2, 0, 32, 6 + 4 * oi)
+        wait_plane(h, OFFS[oi], 2, 32, 32, 7 + 4 * oi)
+
+    def second_stage(oi):
         o = OFFS[oi]
         for h in (0, 1):
             wait_plane(h, o, -1, 0, 64, 4 + 4 * oi)
             send_plane(h, o, -1, 0, 32, 0, 1, 6 + 4 * oi)
             wait_plane(h, o, 1, 0, 64, 5 + 4 * oi)
             send_plane(h, o, 1, 32, 32, 0, -1, 7 + 4 * oi)
-    for i, dx in enumerate((0, -1, 1, 2)):
-        wait_line(lax.rem(x + dx + SIDE, SIDE) * 2 + (1 - core), 0, 128, 4 + i)
-    for oi in range(4):
-        for h in (0, 1):
-            wait_plane(h, OFFS[oi], 2, 0, 32, 6 + 4 * oi)
-            wait_plane(h, OFFS[oi], 2, 32, 32, 7 + 4 * oi)
-    own_c.wait()
-    own_r.wait()
-
-    score_scale = LOG2E / math.sqrt(WIDTH)
-
-    def score_tile(t, carry):
-        n, m = t // 4, t % 4
-        left = er[pl.ds(2 * m, 2)].reshape(2 * BLOCK, WIDTH)
-        right = ec[pl.ds(2 * n, 2)].reshape(2 * BLOCK, WIDTH)
-        out = lax.dot_general(left, right, (((1,), (1,)), ((), ())), preferred_element_type=F32)
-        s[pl.ds(pl.multiple_of(m * 256, 256), 256), pl.ds(pl.multiple_of(n * 256, 256), 256)] = out * score_scale
-        return carry
-
-    lax.fori_loop(0, 32, score_tile, 0)
+
+    score_tile(0, False)
+    second_stage(1)
+    wait_forwarded(1, 0)
+    score_tile(0, True)
+    second_stage(2)
+    score_tile(-1, False)
+    score_tile(1, False)
+    second_stage(3)
+    wait_forwarded(1, 1)
+    wait_forwarded(1, 2)
+    score_tile(-1, True)
+    score_tile(1, True)
+    wait_forwarded(0, 0)
+    wait_forwarded(0, 1)
+    wait_forwarded(0, 2)
+    score_tile(2, False)
+    wait_forwarded(0, 3)
+    wait_forwarded(1, 3)
+    score_tile(2, True)
     eye = lax.broadcasted_iota(jnp.int32, (BLOCK, BLOCK), 0) == lax.broadcasted_iota(jnp.int32, (BLOCK, BLOCK), 1)
     dr = pl.ds(pl.multiple_of(b * BLOCK, BLOCK), BLOCK)
     dc = pl.ds(pl.multiple_of(a * BLOCK, BLOCK), BLOCK)
@@ -196,7 +222,7 @@
             out.append(jnp.sum(v, axis=0, keepdims=True))
         return jnp.concatenate(out, axis=0)
 
-    def exchange(e):
+    def send_cols(e):
         def to_plane(k, carry):
             pltpu.make_async_remote_copy(
                 src_ref=cmsg.at[e], dst_ref=crx.at[e, a], send_sem=csend.at[e], recv_sem=crecv.at[e],
@@ -204,6 +230,10 @@
             ).start()
             return carry
 
+        lax.fori_loop(1, PLANE, to_plane, 0)
+        crx[e, a] = cmsg[e]
+
+    def send_rows(e):
         def to_line(k, carry):
             pltpu.make_async_remote_copy(
                 src_ref=rmsg.at[e], dst_ref=rrx.at[e, b], send_sem=rsend.at[e], recv_sem=rrecv.at[e],
@@ -212,167 +242,206 @@
             return carry
 
         lax.fori_loop(1, LINE, to_line, 0)
-        lax.fori_loop(1, PLANE, to_plane, 0)
-        crx[e, a] = cmsg[e]
         rrx[e, b] = rmsg[e]
-        call = crx.at[e, pl.ds(0, PLANE - 1)]
-        rall = rrx.at[e, pl.ds(0, LINE - 1)]
-        pltpu.make_async_copy(rall, rall, rrecv.at[e]).wait()
-        pltpu.make_async_copy(call, call, crecv.at[e]).wait()
-        pltpu.make_async_copy(rall, rall, rsend.at[e]).wait()
-        pltpu.make_async_copy(call, call, csend.at[e]).wait()
+
+    def wait_cols(e):
+        every = crx.at[e, pl.ds(0, PLANE - 1)]
+        pltpu.make_async_copy(every, every, crecv.at[e]).wait()
+
+    def wait_rows(e):
+        every = rrx.at[e, pl.ds(0, LINE - 1)]
+        pltpu.make_async_copy(every, every, rrecv.at[e]).wait()
 
     def merge(v):
         top = jnp.max(v, axis=0)
         return top + log2(jnp.sum(jnp.exp2(v - top[None]), axis=0))
 
-    def forward(t):
-        pot_r, pot_c = rvec.at[t - 2], cvec.at[t - 2]
-
-        def top_step(i, tops):
+    low = jnp.full((8, BLOCK), -jnp.inf, F32)
+    zero = jnp.zeros((8, BLOCK), F32)
+    steps = RROWS // CH
+
+    def row_lse(t):
+        pot_c = cvec.at[t - 2]
+
+        def step(i, carry):
             rows = rows_at(i)
-            if t > 1:
-                pr = pot_r[rows, :]
-            best = None
-            out = []
-            for k in range(PLANE):
+
+            def value(k):
                 v = s[rows, lanes(k)]
-                u = v + pot_c[k : k + 1, :] if t > 1 else v
-                q = v + pr if t > 1 else v
-                best = u if best is None else jnp.maximum(best, u)
-                out.append(jnp.maximum(tops[k], fold(q, jnp.maximum)))
-            mr[rows, :] = jnp.broadcast_to(jnp.max(best, axis=1, keepdims=True), (CH, BLOCK))
-            return tuple(out)
-
-        low = jnp.full((8, BLOCK), -jnp.inf, F32)
-        tops = lax.fori_loop(0, RROWS // CH, top_step, (low,) * PLANE)
-        ctop = jnp.concatenate([jnp.max(v, axis=0, keepdims=True) for v in tops], axis=0)
-        cvec[7] = ctop
-
-        def sum_step(i, sums):
-            rows = rows_at(i)
-            m = mr[rows, :]
-            if t > 1:
-                pr = pot_r[rows, :]
-            acc = None
-            out = []
-            for k in range(PLANE):
-                v = s[rows, lanes(k)]
-                u = v + pot_c[k : k + 1, :] if t > 1 else v
-                q = v + pr if t > 1 else v
-                p = jnp.exp2(u - m)
-                acc = p if acc is None else acc + p
-                out.append(sums[k] + fold(jnp.exp2(q - cvec[7, k : k + 1, :]), jnp.add))
-            total = jnp.sum(acc, axis=1, keepdims=True)
-            accr[rows, :] = m + log2(jnp.broadcast_to(total, (CH, BLOCK)))
-            return tuple(out)
-
-        zero = jnp.zeros((8, BLOCK), F32)
-        sums = lax.fori_loop(0, RROWS // CH, sum_step, (zero,) * PLANE)
-        csum = jnp.concatenate([jnp.sum(v, axis=0, keepdims=True) for v in sums], axis=0)
-        cmsg[t - 1, 0:PLANE, :] = ctop + log2(csum)
+                return v + pot_c[k : k + 1, :] if t > 1 else v
+
+            best = value(0)
+            for k in range(1, PLANE):
+                best = jnp.maximum(best, value(k))
+            m = jnp.broadcast_to(jnp.max(best, axis=1, keepdims=True), (CH, BLOCK))
+            acc = jnp.exp2(value(0) - m)
+            for k in range(1, PLANE):
+                acc = acc + jnp.exp2(value(k) - m)
+            total = jnp.broadcast_to(jnp.sum(acc, axis=1, keepdims=True), (CH, BLOCK))
+            accr[rows, :] = m + log2(total)
+            return carry
+
+        lax.fori_loop(0, steps, step, 0)
         rmsg[t - 1, 0:LINE, :] = from_rows(accr)
         if t == 1:
             rmsg[0, LINE : LINE + 8, :] = jnp.broadcast_to(pos[...].astype(F32), (8, BLOCK))
-        exchange(t - 1)
-        lse_c = merge(crx[t - 1, :, 0:PLANE, :])
-        lse_r = merge(rrx[t - 1, :, 0:LINE, :])
-        return lse_r, lse_c
+        send_rows(t - 1)
+
+    def col_lse(t):
+        pot_r = rvec.at[t - 2]
+
+        def value(rows, k, pr):
+            v = s[rows, lanes(k)]
+            return v + pr if t > 1 else v
+
+        def top_step(i, tops):
+            rows = rows_at(i)
+            pr = pot_r[rows, :] if t > 1 else None
+            return tuple(jnp.maximum(tops[k], fold(value(rows, k, pr), jnp.maximum)) for k in range(PLANE))
+
+        tops = lax.fori_loop(0, steps, top_step, (low,) * PLANE)
+        ctop = jnp.concatenate([jnp.max(v, axis=0, keepdims=True) for v in tops], axis=0)
+        cvec[7] = ctop
+
+        def sum_step(i, sums):
+            rows = rows_at(i)
+            pr = pot_r[rows, :] if t > 1 else None
+            return tuple(
+                sums[k] + fold(jnp.exp2(value(rows, k, pr) - cvec[7, k : k + 1, :]), jnp.add) for k in range(PLANE)
+            )
+
+        sums = lax.fori_loop(0, steps, sum_step, (zero,) * PLANE)
+        csum = jnp.concatenate([jnp.sum(v, axis=0, keepdims=True) for v in sums], axis=0)
+        cmsg[t - 1, 0:PLANE, :] = ctop + log2(csum)
+        send_cols(t - 1)
 
     cmsg[...] = jnp.zeros_like(cmsg)
     rmsg[...] = jnp.zeros_like(rmsg)
+    row_lse(1)
+    col_lse(1)
+    wait_rows(0)
+    to_rows(jnp.concatenate([rrx[0, g, LINE : LINE + 1, :] for g in range(LINE)], axis=0), pr_ref)
     pot_r = jnp.zeros((LINE, BLOCK), F32)
     pot_c = jnp.zeros((PLANE, BLOCK), F32)
-    for t in (1, 2, 3):
-        lse_r, lse_c = forward(t)
+    for t in (1, 2):
+        if t > 1:
+            wait_rows(t - 1)
+        lse_r = merge(rrx[t - 1, :, 0:LINE, :])
         pot_r = (pot_r - lse_r) * 0.5
+        to_rows(lse_r, rvec.at[t + 1])
+        to_rows(pot_r, rvec.at[t - 1])
+        col_lse(t + 1)
+        wait_cols(t - 1)
+        lse_c = merge(crx[t - 1, :, 0:PLANE, :])
         pot_c = (pot_c - lse_c) * 0.5
-        to_rows(lse_r, rvec.at[t + 1])
         cvec[t + 1] = lse_c
-        if t < 3:
-            to_rows(pot_r, rvec.at[t - 1])
-            cvec[t - 1] = pot_c
-        if t == 1:
-            to_rows(jnp.concatenate([rrx[0, g, LINE : LINE + 1, :] for g in range(LINE)], axis=0), pr_ref)
+        cvec[t - 1] = pot_c
+        row_lse(t + 1)
 
     first_col = (lax.broadcasted_iota(jnp.int32, (8, BLOCK), 1) + b * BLOCK).astype(F32)
     first_col = jnp.broadcast_to(first_col[0:1], (CH, BLOCK))
 
-    def backward(t):
-        pot_rr, pot_cc = rvec.at[t - 2], cvec.at[t - 2]
-        lse_rr, lse_cc = rvec.at[t + 1], cvec.at[t + 1]
-        pull_rr, pull_cc = rvec.at[7 - t], cvec.at[7 - t]
+    def add_term(t):
+        pot_cc, lse_rr, pull_rr = cvec.at[t - 2], rvec.at[t + 1], rvec.at[7 - t]
 
         def step(i, carry):
             sums, picked = carry
             rows = rows_at(i)
             lr = lse_rr[rows, :]
-            if t > 1:
-                pr = pot_rr[rows, :]
             if t < 3:
                 qr = pull_rr[rows, :]
             else:
                 partner = pr_ref[rows, :] - first_col
-            acc = None
             out = []
             for k in range(PLANE):
                 v = s[rows, lanes(k)]
                 u = v + pot_cc[k : k + 1, :] if t > 1 else v
-                q = v + pr if t > 1 else v
                 term = jnp.exp2(u - lr)
-                mirror = jnp.exp2(q - lse_cc[k : k + 1, :])
                 if t < 3:
                     term = term * qr
-                    mirror = mirror * pull_cc[k : k + 1, :]
-                    total = w[rows, lanes(k)] + (term + mirror)
+                    w[rows, lanes(k)] = w[rows, lanes(k)] + term
                 else:
                     hit = partner == float(k * RROWS)
                     picked = picked + fold(jnp.where(hit, v, 0.0), jnp.add)
-                    total = jnp.where(hit, -2.0, 0.0) + (term + mirror)
+                    w[rows, lanes(k)] = jnp.where(hit, term - 2.0, term)
+                if t > 1:
+                    out.append(sums[k] + fold(term, jnp.add))
+            return tuple(out), picked
+
+        return lax.fori_loop(0, steps, step, ((zero,) * (PLANE if t > 1 else 0), zero))
+
+    def add_mirror(t, start=0, count=steps):
+        pot_rr, lse_cc, pull_cc = rvec.at[t - 2], cvec.at[t + 1], cvec.at[7 - t]
+
+        def step(i, carry):
+            rows = rows_at(start + i)
+            if t > 1:
+                pr = pot_rr[rows, :]
+            acc = None
+            for k in range(PLANE):
+                v = s[rows, lanes(k)]
+                q = v + pr if t > 1 else v
+                mirror = jnp.exp2(q - lse_cc[k : k + 1, :])
+                if t < 3:
+                    mirror = mirror * pull_cc[k : k + 1, :]
+                total = w[rows, lanes(k)] + mirror
                 if t > 1:
                     w[rows, lanes(k)] = total
-                    out.append(sums[k] + fold(term, jnp.add))
                     acc = mirror if acc is None else acc + mirror
                 else:
                     wb[rows, lanes(k)] = total.astype(BF16)
             if t > 1:
                 accr[rows, :] = jnp.broadcast_to(jnp.sum(acc, axis=1, keepdims=True), (CH, BLOCK))
-            return tuple(out), picked
-
-        zero = jnp.zeros((8, BLOCK), F32)
-        sums, picked = lax.fori_loop(0, RROWS // CH, step, ((zero,) * (PLANE if t > 1 else 0), zero))
-        if t == 1:
-            return None
-        e = 6 - t
+            return carry
+
+        lax.fori_loop(0, count, step, 0)
+
+    def col_sums(e, sums):
         cmsg[e, 0:PLANE, :] = jnp.concatenate([jnp.sum(v, axis=0, keepdims=True) for v in sums], axis=0)
-        rmsg[e, 0:LINE, :] = from_rows(accr)
-        if t == 3:
-            cmsg[e, PLANE : PLANE + 8, :] = picked
-        return e
-
-    e = backward(3)
-    exchange(e)
-    cot_r = -1.0 + jnp.sum(rrx[e, :, 0:LINE, :], axis=0)
-    cot_c = -1.0 + jnp.sum(crx[e, :, 0:PLANE, :], axis=0)
-    picked = jnp.sum(crx[e, :, PLANE : PLANE + 8, :], axis=0)
+        send_cols(e)
+
+    wait_rows(2)
+    lse_r = merge(rrx[2, :, 0:LINE, :])
+    to_rows(lse_r, rvec.at[4])
+    sums, picked = add_term(3)
+    cmsg[3, PLANE : PLANE + 8, :] = picked
+    col_sums(3, sums)
+    wait_cols(2)
+    lse_c = merge(crx[2, :, 0:PLANE, :])
+    cvec[4] = lse_c
+    pot_c = (pot_c - lse_c) * 0.5
+    add_mirror(3)
+    rmsg[3, 0:LINE, :] = from_rows(accr)
+    send_rows(3)
+    wait_rows(3)
+    cot_r = -1.0 + jnp.sum(rrx[3, :, 0:LINE, :], axis=0)
     to_rows(-0.5 * cot_r, rvec.at[5])
+    sums, _ = add_term(2)
+    col_sums(4, sums)
+    wait_cols(3)
+    cot_c = -1.0 + jnp.sum(crx[3, :, 0:PLANE, :], axis=0)
     cvec[5] = -0.5 * cot_c
-    e = backward(2)
-    rmsg[e, LINE : LINE + 8, :] = picked + 2.0 * (pot_c[0:8] + pot_c[8:16])
-    exchange(e)
-    cot_r = 0.5 * cot_r + jnp.sum(rrx[e, :, 0:LINE, :], axis=0)
-    cot_c = 0.5 * cot_c + jnp.sum(crx[e, :, 0:PLANE, :], axis=0)
-    whole = jnp.sum(rrx[e, :, LINE : LINE + 8, :], axis=0)
+    picked = jnp.sum(crx[3, :, PLANE : PLANE + 8, :], axis=0)
+    rmsg[4, LINE : LINE + 8, :] = picked + 2.0 * (pot_c[0:8] + pot_c[8:16])
+    add_mirror(2)
+    rmsg[4, 0:LINE, :] = from_rows(accr)
+    send_rows(4)
+    wait_rows(4)
+    cot_r = 0.5 * cot_r + jnp.sum(rrx[4, :, 0:LINE, :], axis=0)
+    whole = jnp.sum(rrx[4, :, LINE : LINE + 8, :], axis=0)
     loss[0, 0] = jnp.sum(whole) * (-LN2 / TOTAL)
     to_rows(-0.5 * cot_r, rvec.at[6])
+    add_term(1)
+    wait_cols(4)
+    cot_c = 0.5 * cot_c + jnp.sum(crx[4, :, 0:PLANE, :], axis=0)
     cvec[6] = -0.5 * cot_c
-    backward(1)
 
     grad_scale = 1.0 / math.sqrt(WIDTH)
 
     def partial(d):
         xx = lax.rem(x + d, SIDE)
         rows = pl.ds(pl.multiple_of(xx * 256, 256), 256)
+        add_mirror(1, xx * (256 // CH), 256 // CH)
 
         def tile(n, carry):
             cols = pl.ds(pl.multiple_of(n * 256, 256), 256)
@@ -429,6 +498,11 @@
     pltpu.make_async_copy(sent, sent, psend).wait()
     sent = er.at[pl.ds(0, LINE - 1)]
     pltpu.make_async_copy(sent, sent, xsend).wait()
+    for e in range(5):
+        every = rrx.at[e, pl.ds(0, LINE - 1)]
+        pltpu.make_async_copy(every, every, rsend.at[e]).wait()
+        every = crx.at[e, pl.ds(0, PLANE - 1)]
+        pltpu.make_async_copy(every, every, csend.at[e]).wait()
     for d in range(SIDE):
         pltpu.make_async_copy(rb.at[d], rb.at[d], gsend.at[d]).wait()
     for c in far + near:

time: 133 us -> 122 us (0.917)
  Pallas kernels: 128 us -> 118 us
    pallas_call x1, Pallas kernels: 128 us -> 118 us  [shards(): pl.pallas_call(kernel, out_shape=(jax.ShapeDtypeStruct((BLOCK, WIDTH), F3...]
where the time goes in v2:
time: 122 us
  Pallas kernels  118 us (97%)
  between operations  2.33 us (2%)
  local copies, waits for them, and re-layouts  1.89 us (2%)
    pallas_call x1, Pallas kernels, shards(): pl.pallas_call(kernel, out_shape=(jax.ShapeDtypeStruct((BLOCK, WIDTH), F3...  118 us

profile of v2, /device:TPU:1, one launch (start us, length us, event | category | flops | bytes accessed | tf_op | source)
XLA Modules:
  0.0 122.0 jit_solution(8662152920583671845)
XLA Ops:
  0.6 117.8 %shard_map.41 = (f32[128,1024]{1,0:T(8,128)}, f32[1,1]{1,0:T(1,128)}) custom-call(bf16[128,1024]{1,0:T(8,128)(2,1)} %emb.1, s32[1,128]{1,0:T(1,128)} %bitcast.2), custom_call_target="tpu_custom_call" | custom-call | tf_op jit(solution)/shard_map/pallas_call | solution.py:515
  119.0 1.9 %copy.7 = f32[128,1024]{1,0:T(8,128)} copy(f32[128,1024]{1,0:T(8,128)} %get-tuple-element.9) | data formatting | bytes 1048576

commit v3 on v2

--- a/solution.py
+++ b/solution.py
@@ -21,9 +21,13 @@
 MESH = pl.DeviceIdType.MESH
 F32 = jnp.float32
 BF16 = jnp.bfloat16
+TILE = 256
 SCORE_M = 4
 CH = 32
 OFFS = (0, -1, 1, 2)
+FAR_FIRST = sorted(
+    ((dy, dz) for dy in OFFS for dz in OFFS if (dy, dz) != (0, 0)), key=lambda d: -abs(d[0]) - abs(d[1])
+)
 
 
 def fold(v, op):
@@ -31,6 +35,12 @@
     for r in range(8, v.shape[0], 8):
         out = op(out, v[r : r + 8])
     return out
+
+
+def tree(v, op):
+    while len(v) > 1:
+        v = [op(*v[i : i + 2]) if i + 1 < len(v) else v[i] for i in range(0, len(v), 2)]
+    return v[0]
 
 
 def log2(v):
@@ -48,12 +58,6 @@
     b = me % LINE
     y, z = a // SIDE, a % SIDE
     x, core = b // 2, b % 2
-
-    def in_plane(k):
-        return lax.rem(a + k, PLANE) * LINE + b
-
-    def in_line(k):
-        return a * LINE + lax.rem(b + k, LINE)
 
     def dev_of(dy, dz, dx, c):
         yy, zz, xx = (lax.rem(v + d + SIDE, SIDE) for v, d in ((y, dy), (z, dz), (x, dx)))
@@ -215,33 +219,24 @@
         for g in range(LINE):
             ref[pl.ds(g * BLOCK, BLOCK), :] = jnp.broadcast_to(v[g : g + 1], (BLOCK, BLOCK)).T
 
-    def from_rows(ref):
-        out = []
-        for g in range(LINE):
-            v = jnp.where(eye, ref[pl.ds(g * BLOCK, BLOCK), :], 0.0)
-            out.append(jnp.sum(v, axis=0, keepdims=True))
+    def row_sums(ref):
+        out = [jnp.sum(ref[pl.ds(g * BLOCK, BLOCK), :].T, axis=0, keepdims=True) for g in range(LINE)]
         return jnp.concatenate(out, axis=0)
 
     def send_cols(e):
-        def to_plane(k, carry):
+        for dy, dz in FAR_FIRST:
             pltpu.make_async_remote_copy(
                 src_ref=cmsg.at[e], dst_ref=crx.at[e, a], send_sem=csend.at[e], recv_sem=crecv.at[e],
-                device_id=(in_plane(k),), device_id_type=MESH,
+                device_id=(dev_of(dy, dz, 0, core),), device_id_type=MESH,
             ).start()
-            return carry
-
-        lax.fori_loop(1, PLANE, to_plane, 0)
         crx[e, a] = cmsg[e]
 
     def send_rows(e):
-        def to_line(k, carry):
+        for dx, other in ((2, 1), (2, 0), (1, 1), (-1, 1), (1, 0), (-1, 0), (0, 1)):
             pltpu.make_async_remote_copy(
                 src_ref=rmsg.at[e], dst_ref=rrx.at[e, b], send_sem=rsend.at[e], recv_sem=rrecv.at[e],
-                device_id=(in_line(k),), device_id_type=MESH,
+                device_id=(dev_of(0, 0, dx, 1 - core if other else core),), device_id_type=MESH,
             ).start()
-            return carry
-
-        lax.fori_loop(1, LINE, to_line, 0)
         rrx[e, b] = rmsg[e]
 
     def wait_cols(e):
@@ -265,24 +260,22 @@
 
         def step(i, carry):
             rows = rows_at(i)
-
-            def value(k):
-                v = s[rows, lanes(k)]
-                return v + pot_c[k : k + 1, :] if t > 1 else v
-
-            best = value(0)
-            for k in range(1, PLANE):
-                best = jnp.maximum(best, value(k))
-            m = jnp.broadcast_to(jnp.max(best, axis=1, keepdims=True), (CH, BLOCK))
-            acc = jnp.exp2(value(0) - m)
-            for k in range(1, PLANE):
-                acc = acc + jnp.exp2(value(k) - m)
-            total = jnp.broadcast_to(jnp.sum(acc, axis=1, keepdims=True), (CH, BLOCK))
-            accr[rows, :] = m + log2(total)
+            v = [s[rows, lanes(k)] for k in range(PLANE)]
+            if t > 1:
+                v = [v[k] + pot_c[k : k + 1, :] for k in range(PLANE)]
+            best = tree(v, jnp.maximum)
+            mr[rows, :] = best
+            accr[rows, :] = tree([jnp.exp2(u - best) for u in v], jnp.add)
             return carry
 
         lax.fori_loop(0, steps, step, 0)
-        rmsg[t - 1, 0:LINE, :] = from_rows(accr)
+        out = []
+        for g in range(LINE):
+            best = mr[pl.ds(g * BLOCK, BLOCK), :].T
+            acc = accr[pl.ds(g * BLOCK, BLOCK), :].T
+            top = jnp.max(best, axis=0, keepdims=True)
+            out.append(top + log2(jnp.sum(acc * jnp.exp2(best - top), axis=0, keepdims=True)))
+        rmsg[t - 1, 0:LINE, :] = jnp.concatenate(out, axis=0)
         if t == 1:
             rmsg[0, LINE : LINE + 8, :] = jnp.broadcast_to(pos[...].astype(F32), (8, BLOCK))
         send_rows(t - 1)
@@ -391,7 +384,7 @@
                 else:
                     wb[rows, lanes(k)] = total.astype(BF16)
             if t > 1:
-                accr[rows, :] = jnp.broadcast_to(jnp.sum(acc, axis=1, keepdims=True), (CH, BLOCK))
+                accr[rows, :] = acc
             return carry
 
         lax.fori_loop(0, count, step, 0)
@@ -411,7 +404,7 @@
     cvec[4] = lse_c
     pot_c = (pot_c - lse_c) * 0.5
     add_mirror(3)
-    rmsg[3, 0:LINE, :] = from_rows(accr)
+    rmsg[3, 0:LINE, :] = row_sums(accr)
     send_rows(3)
     wait_rows(3)
     cot_r = -1.0 + jnp.sum(rrx[3, :, 0:LINE, :], axis=0)
@@ -424,7 +417,7 @@
     picked = jnp.sum(crx[3, :, PLANE : PLANE + 8, :], axis=0)
     rmsg[4, LINE : LINE + 8, :] = picked + 2.0 * (pot_c[0:8] + pot_c[8:16])
     add_mirror(2)
-    rmsg[4, 0:LINE, :] = from_rows(accr)
+    rmsg[4, 0:LINE, :] = row_sums(accr)
     send_rows(4)
     wait_rows(4)
     cot_r = 0.5 * cot_r + jnp.sum(rrx[4, :, 0:LINE, :], axis=0)
@@ -438,61 +431,73 @@
 
     grad_scale = 1.0 / math.sqrt(WIDTH)
 
-    def partial(d):
-        xx = lax.rem(x + d, SIDE)
-        rows = pl.ds(pl.multiple_of(xx * 256, 256), 256)
-        add_mirror(1, xx * (256 // CH), 256 // CH)
-
-        def tile(n, carry):
-            cols = pl.ds(pl.multiple_of(n * 256, 256), 256)
-            right = ec[:, :, cols].reshape(CCOLS, 256)
-            out = jnp.dot(wb[rows, :], right, preferred_element_type=F32) * grad_scale
-            gp[d, :, :, cols] = out.reshape(2, BLOCK, 256)
-            return carry
-
-        lax.fori_loop(0, WIDTH // 256, tile, 0)
+    add_mirror(1)
+
+    def product(n):
+        right = ec[:, :, pl.ds(n * TILE, TILE)].reshape(CCOLS, TILE)
+        for m in range(2):
+            out = jnp.dot(wb[pl.ds(m * 512, 512), :], right, preferred_element_type=F32) * grad_scale
+            for g in range(4):
+                block = 4 * m + g
+                gp[n, block % 2, block // 2] = out[g * BLOCK : (g + 1) * BLOCK]
         pltpu.make_async_remote_copy(
-            src_ref=gp.at[d, 1 - core], dst_ref=rb.at[d], send_sem=gsend.at[d], recv_sem=grecv.at[d],
+            src_ref=gp.at[n, 1 - core], dst_ref=rb.at[n], send_sem=gsend.at[n], recv_sem=grecv.at[n],
             device_id=(sibling,), device_id_type=MESH,
         ).start()
 
-    def chip_sum(d):
-        pltpu.make_async_copy(rb.at[d], rb.at[d], grecv.at[d]).wait()
-        return gp[d, core] + rb[d]
-
-    def ring(src, dst, i, device):
+    def ring(src, dst, i, dx):
         return pltpu.make_async_remote_copy(
             src_ref=src, dst_ref=dst, send_sem=hsend.at[i], recv_sem=hrecv.at[i],
-            device_id=(device,), device_id_type=MESH,
+            device_id=(xdev(dx),), device_id_type=MESH,
         )
 
-    half = WIDTH // 2
-    far = [ring(xs2.at[i], xr2.at[i], i, xdev(dx)) for i, dx in ((0, 1), (1, -1))]
-    near = [ring(xs1.at[i], xr1.at[i], 2 + i, xdev(dx)) for i, dx in ((0, 1), (1, -1))]
-    partial(2)
-    partial(1)
-    v = chip_sum(2).astype(BF16)
-    xs2[0] = v[:, :half]
-    xs2[1] = v[:, half:]
-    far[0].start()
-    far[1].start()
-    partial(3)
-    v = chip_sum(1)
-    far[0].wait_recv()
-    xs1[0, :, :half] = (v[:, :half] + xr2[0].astype(F32)).astype(BF16)
-    xs1[0, :, half:] = v[:, half:].astype(BF16)
-    near[0].start()
-    partial(0)
-    v = chip_sum(3)
-    far[1].wait_recv()
-    xs1[1, :, :half] = v[:, :half].astype(BF16)
-    xs1[1, :, half:] = (v[:, half:] + xr2[1].astype(F32)).astype(BF16)
-    near[1].start()
-    v = chip_sum(0)
-    near[0].wait_recv()
-    v = v + xr1[0].astype(F32)
-    near[1].wait_recv()
-    grad[...] = v + xr1[1].astype(F32)
+    half = TILE // 2
+    first = [[ring(xs1.at[n, i], xr1.at[n, i], 4 * n + i, dx) for i, dx in ((0, 1), (1, -1))] for n in range(SIDE)]
+    second = [[ring(xs2.at[n, i], xr2.at[n, i], 4 * n + 2 + i, dx) for i, dx in ((0, 1), (1, -1))] for n in range(SIDE)]
+
+    def chip_sum(n, d):
+        xx = lax.rem(x + d, SIDE)
+        return gp[n, core, xx] + rb[n, xx]
+
+    def send_first(n):
+        pltpu.make_async_copy(rb.at[n], rb.at[n], grecv.at[n]).wait()
+        far = chip_sum(n, 2).astype(BF16)
+        xs1[n, 0, :, :half] = far[:, :half]
+        xs1[n, 0, :, half:] = chip_sum(n, 1)[:, half:].astype(BF16)
+        first[n][0].start()
+        xs1[n, 1, :, half:] = far[:, half:]
+        xs1[n, 1, :, :half] = chip_sum(n, 3)[:, :half].astype(BF16)
+        first[n][1].start()
+
+    def send_second(n):
+        first[n][0].wait_recv()
+        xs2[n, 0] = (chip_sum(n, 1)[:, :half] + xr1[n, 0, :, :half].astype(F32)).astype(BF16)
+        second[n][0].start()
+        first[n][1].wait_recv()
+        xs2[n, 1] = (chip_sum(n, 3)[:, half:] + xr1[n, 1, :, half:].astype(F32)).astype(BF16)
+        second[n][1].start()
+
+    def finish(n):
+        own = chip_sum(n, 0)
+        second[n][0].wait_recv()
+        second[n][1].wait_recv()
+        lo, mid = n * TILE, n * TILE + half
+        grad[:, lo:mid] = own[:, :half] + xr2[n, 0].astype(F32) + xr1[n, 1, :, :half].astype(F32)
+        grad[:, mid : mid + half] = own[:, half:] + xr2[n, 1].astype(F32) + xr1[n, 0, :, half:].astype(F32)
+
+    for n in range(SIDE):
+        product(n)
+        if n >= 1:
+            send_first(n - 1)
+        if n >= 2:
+            send_second(n - 2)
+    send_first(3)
+    send_second(2)
+    finish(0)
+    finish(1)
+    send_second(3)
+    finish(2)
+    finish(3)
 
     sent = ec.at[pl.ds(0, PLANE - 1)]
     pltpu.make_async_copy(sent, sent, psend).wait()
@@ -505,7 +510,7 @@
         pltpu.make_async_copy(every, every, csend.at[e]).wait()
     for d in range(SIDE):
         pltpu.make_async_copy(rb.at[d], rb.at[d], gsend.at[d]).wait()
-    for c in far + near:
+    for c in sum(first + second, []):
         c.wait_send()
 
 
@@ -535,12 +540,12 @@
             vec((5, PLANE, PLANE + 8, BLOCK), F32),
             vec((5, LINE + 8, BLOCK), F32),
             vec((5, LINE, LINE + 8, BLOCK), F32),
-            vec((SIDE, 2, BLOCK, WIDTH), F32),
-            vec((SIDE, BLOCK, WIDTH), F32),
-            vec((2, BLOCK, WIDTH // 2), BF16),
-            vec((2, BLOCK, WIDTH // 2), BF16),
-            vec((2, BLOCK, WIDTH), BF16),
-            vec((2, BLOCK, WIDTH), BF16),
+            vec((SIDE, 2, SIDE, BLOCK, TILE), F32),
+            vec((SIDE, SIDE, BLOCK, TILE), F32),
+            vec((SIDE, 2, BLOCK, TILE // 2), BF16),
+            vec((SIDE, 2, BLOCK, TILE // 2), BF16),
+            vec((SIDE, 2, BLOCK, TILE), BF16),
+            vec((SIDE, 2, BLOCK, TILE), BF16),
             dma((2,)),
             dma,
             dma((2, 20)),
@@ -552,8 +557,8 @@
             dma((5,)),
             dma((SIDE,)),
             dma((SIDE,)),
-            dma((4,)),
-            dma((4,)),
+            dma((16,)),
+            dma((16,)),
         ],
         compiler_params=pltpu.CompilerParams(
             collective_id=0, has_side_effects=True, vmem_limit_bytes=56 * 1024 * 1024

time: 122 us -> 102 us (0.84)
  Pallas kernels: 118 us -> 97.4 us
    pallas_call x1, Pallas kernels: 118 us -> 97.4 us  [shards(): pl.pallas_call(kernel, out_shape=(jax.ShapeDtypeStruct((BLOCK, WIDTH), F3...]
where the time goes in v3:
time: 102 us
  Pallas kernels  97.4 us (95%)
  between operations  2.33 us (2%)
  local copies, waits for them, and re-layouts  1.89 us (2%)
    pallas_call x1, Pallas kernels, shards(): pl.pallas_call(kernel, out_shape=(jax.ShapeDtypeStruct((BLOCK, WIDTH), F3...  97.4 us

profile of v3, /device:TPU:1, one launch (start us, length us, event | category | flops | bytes accessed | tf_op | source)
XLA Modules:
  0.0 101.6 jit_solution(15761239842792227106)
XLA Ops:
  0.6 97.4 %shard_map.41 = (f32[128,1024]{1,0:T(8,128)}, f32[1,1]{1,0:T(1,128)}) custom-call(bf16[128,1024]{1,0:T(8,128)(2,1)} %emb.1, s32[1,128]{1,0:T(1,128)} %bitcast.2), custom_call_target="tpu_custom_call" | custom-call | tf_op jit(solution)/shard_map/pallas_call | solution.py:520
  98.6 1.9 %copy.7 = f32[128,1024]{1,0:T(8,128)} copy(f32[128,1024]{1,0:T(8,128)} %get-tuple-element.9) | data formatting | bytes 1048576

commit v4 on v3

--- a/solution.py
+++ b/solution.py
@@ -23,7 +23,7 @@
 BF16 = jnp.bfloat16
 TILE = 256
 SCORE_M = 4
-CH = 32
+CH = 64
 OFFS = (0, -1, 1, 2)
 FAR_FIRST = sorted(
     ((dy, dz) for dy in OFFS for dz in OFFS if (dy, dz) != (0, 0)), key=lambda d: -abs(d[0]) - abs(d[1])
@@ -31,10 +31,7 @@
 
 
 def fold(v, op):
-    out = v[0:8]
-    for r in range(8, v.shape[0], 8):
-        out = op(out, v[r : r + 8])
-    return out
+    return tree([v[r : r + 8] for r in range(0, v.shape[0], 8)], op)
 
 
 def tree(v, op):
@@ -50,8 +47,8 @@
 def kernel(
     emb, pos, grad, loss,
     ec, er, s, w, wb, rvec, cvec, pr_ref, mr, accr, cmsg, crx, rmsg, rrx,
-    gp, rb, xs2, xr2, xs1, xr1,
-    lsem, psend, prsem, xsend, xrsem, csend, crecv, rsend, rrecv, gsend, grecv, hsend, hrecv,
+    lmsg, lrx, gp, rb, xs2, xr2, xs1, xr1,
+    lsem, psend, prsem, xsend, xrsem, csend, crecv, rsend, rrecv, losem, gsend, grecv, hsend, hrecv,
 ):
     me = lax.axis_index("dp")
     a = me // LINE
@@ -157,6 +154,14 @@
     own_c.wait()
     own_r.wait()
 
+    eye = lax.broadcasted_iota(jnp.int32, (BLOCK, BLOCK), 0) == lax.broadcasted_iota(jnp.int32, (BLOCK, BLOCK), 1)
+    low = jnp.full((8, BLOCK), -3e38, F32)
+    zero = jnp.zeros((8, BLOCK), F32)
+    steps = RROWS // CH
+
+    def rows_at(i):
+        return pl.ds(pl.multiple_of(i * CH, CH), CH)
+
     score_scale = LOG2E / math.sqrt(WIDTH)
 
     def score_tile(dy, other):
@@ -172,6 +177,40 @@
             return carry
 
         lax.fori_loop(0, LINE // SCORE_M, part, 0)
+        if dy == 0 and not other:
+            dr = pl.ds(pl.multiple_of(b * BLOCK, BLOCK), BLOCK)
+            dc = pl.ds(pl.multiple_of(a * BLOCK, BLOCK), BLOCK)
+            s[dr, dc] = jnp.where(eye, -30000.0 * LOG2E, s[dr, dc])
+        first_sums(n, dy == 0 and not other)
+
+    def first_sums(n, fresh):
+        two = [pl.ds(pl.multiple_of(n * 256 + k * BLOCK, BLOCK), BLOCK) for k in range(2)]
+
+        def step(i, carry):
+            rows = rows_at(i)
+            v = [s[rows, c] for c in two]
+            top = jnp.maximum(v[0], v[1])
+            if not fresh:
+                old = mr[rows, :]
+                top = jnp.maximum(top, old)
+            acc = jnp.exp2(v[0] - top) + jnp.exp2(v[1] - top)
+            if not fresh:
+                acc = acc + accr[rows, :] * jnp.exp2(old - top)
+            mr[rows, :] = top
+            accr[rows, :] = acc
+            out = []
+            for k in range(2):
+                old, acc = carry[k]
+                top = jnp.maximum(old, fold(v[k], jnp.maximum))
+                p = [jnp.exp2(v[k][r : r + 8] - top) for r in range(0, CH, 8)]
+                out.append((top, acc * jnp.exp2(old - top) + tree(p, jnp.add)))
+            return tuple(out)
+
+        sums = lax.fori_loop(0, steps, step, ((low, zero),) * 2)
+        for k in range(2):
+            each, acc = sums[k]
+            top = jnp.max(each, axis=0, keepdims=True)
+            cmsg[0, pl.ds(2 * n + k, 1), :] = top + log2(jnp.sum(acc * jnp.exp2(each - top), axis=0, keepdims=True))
 
     def wait_forwarded(h, oi):
         wait_plane(h, OFFS[oi], 2, 0, 32, 6 + 4 * oi)
@@ -204,14 +243,6 @@
     wait_forwarded(0, 3)
     wait_forwarded(1, 3)
     score_tile(2, True)
-    eye = lax.broadcasted_iota(jnp.int32, (BLOCK, BLOCK), 0) == lax.broadcasted_iota(jnp.int32, (BLOCK, BLOCK), 1)
-    dr = pl.ds(pl.multiple_of(b * BLOCK, BLOCK), BLOCK)
-    dc = pl.ds(pl.multiple_of(a * BLOCK, BLOCK), BLOCK)
-    s[dr, dc] = jnp.where(eye, -30000.0 * LOG2E, s[dr, dc])
-
-    def rows_at(i):
-        return pl.ds(pl.multiple_of(i * CH, CH), CH)
-
     def lanes(k):
         return slice(k * BLOCK, (k + 1) * BLOCK)
 
@@ -247,28 +278,36 @@
         every = rrx.at[e, pl.ds(0, LINE - 1)]
         pltpu.make_async_copy(every, every, rrecv.at[e]).wait()
 
+    def send_loss():
+        for dy, dz in FAR_FIRST:
+            pltpu.make_async_remote_copy(
+                src_ref=lmsg, dst_ref=lrx.at[a], send_sem=losem.at[0], recv_sem=losem.at[1],
+                device_id=(dev_of(dy, dz, 0, core),), device_id_type=MESH,
+            ).start()
+        lrx[a] = lmsg[...]
+
     def merge(v):
         top = jnp.max(v, axis=0)
         return top + log2(jnp.sum(jnp.exp2(v - top[None]), axis=0))
 
-    low = jnp.full((8, BLOCK), -jnp.inf, F32)
-    zero = jnp.zeros((8, BLOCK), F32)
-    steps = RROWS // CH
-
     def row_lse(t):
         pot_c = cvec.at[t - 2]
 
         def step(i, carry):
             rows = rows_at(i)
-            v = [s[rows, lanes(k)] for k in range(PLANE)]
-            if t > 1:
-                v = [v[k] + pot_c[k : k + 1, :] for k in range(PLANE)]
-            best = tree(v, jnp.maximum)
+            best = tree([s[rows, lanes(k)] + pot_c[k : k + 1, :] for k in range(PLANE)], jnp.maximum)
             mr[rows, :] = best
-            accr[rows, :] = tree([jnp.exp2(u - best) for u in v], jnp.add)
+            acc = None
+            for k in range(PLANE):
+                p = jnp.exp2(s[rows, lanes(k)] + pot_c[k : k + 1, :] - best)
+                acc = p if acc is None else acc + p
+            accr[rows, :] = acc
             return carry
 
         lax.fori_loop(0, steps, step, 0)
+        send_row_lse(t)
+
+    def send_row_lse(t):
         out = []
         for g in range(LINE):
             best = mr[pl.ds(g * BLOCK, BLOCK), :].T
@@ -276,20 +315,17 @@
             top = jnp.max(best, axis=0, keepdims=True)
             out.append(top + log2(jnp.sum(acc * jnp.exp2(best - top), axis=0, keepdims=True)))
         rmsg[t - 1, 0:LINE, :] = jnp.concatenate(out, axis=0)
-        if t == 1:
-            rmsg[0, LINE : LINE + 8, :] = jnp.broadcast_to(pos[...].astype(F32), (8, BLOCK))
         send_rows(t - 1)
 
     def col_lse(t):
         pot_r = rvec.at[t - 2]
 
         def value(rows, k, pr):
-            v = s[rows, lanes(k)]
-            return v + pr if t > 1 else v
+            return s[rows, lanes(k)] + pr
 
         def top_step(i, tops):
             rows = rows_at(i)
-            pr = pot_r[rows, :] if t > 1 else None
+            pr = pot_r[rows, :]
             return tuple(jnp.maximum(tops[k], fold(value(rows, k, pr), jnp.maximum)) for k in range(PLANE))
 
         tops = lax.fori_loop(0, steps, top_step, (low,) * PLANE)
@@ -298,38 +334,49 @@
 
         def sum_step(i, sums):
             rows = rows_at(i)
-            pr = pot_r[rows, :] if t > 1 else None
+            pr = pot_r[rows, :]
             return tuple(
                 sums[k] + fold(jnp.exp2(value(rows, k, pr) - cvec[7, k : k + 1, :]), jnp.add) for k in range(PLANE)
             )
 
         sums = lax.fori_loop(0, steps, sum_step, (zero,) * PLANE)
         csum = jnp.concatenate([jnp.sum(v, axis=0, keepdims=True) for v in sums], axis=0)
-        cmsg[t - 1, 0:PLANE, :] = ctop + log2(csum)
+        cmsg[t - 1] = ctop + log2(csum)
         send_cols(t - 1)
 
-    cmsg[...] = jnp.zeros_like(cmsg)
+    def take_rows(e):
+        wait_rows(e)
+        return merge(rrx[e, :, 0:LINE, :])
+
+    def take_cols(e):
+        wait_cols(e)
+        return merge(crx[e])
+
     rmsg[...] = jnp.zeros_like(rmsg)
-    row_lse(1)
-    col_lse(1)
-    wait_rows(0)
+    rmsg[0, LINE : LINE + 8, :] = jnp.broadcast_to(pos[...].astype(F32), (8, BLOCK))
+    send_cols(0)
+    send_row_lse(1)
+    lse_r = take_rows(0)
+    pot_r = -0.5 * lse_r
+    to_rows(pot_r, rvec.at[0])
+    col_lse(2)
+    to_rows(lse_r, rvec.at[2])
     to_rows(jnp.concatenate([rrx[0, g, LINE : LINE + 1, :] for g in range(LINE)], axis=0), pr_ref)
-    pot_r = jnp.zeros((LINE, BLOCK), F32)
-    pot_c = jnp.zeros((PLANE, BLOCK), F32)
-    for t in (1, 2):
-        if t > 1:
-            wait_rows(t - 1)
-        lse_r = merge(rrx[t - 1, :, 0:LINE, :])
-        pot_r = (pot_r - lse_r) * 0.5
-        to_rows(lse_r, rvec.at[t + 1])
-        to_rows(pot_r, rvec.at[t - 1])
-        col_lse(t + 1)
-        wait_cols(t - 1)
-        lse_c = merge(crx[t - 1, :, 0:PLANE, :])
-        pot_c = (pot_c - lse_c) * 0.5
-        cvec[t + 1] = lse_c
-        cvec[t - 1] = pot_c
-        row_lse(t + 1)
+    lse_c = take_cols(0)
+    pot_c = -0.5 * lse_c
+    cvec[2] = lse_c
+    cvec[0] = pot_c
+    row_lse(2)
+    lse_c = take_cols(1)
+    pot_c = (pot_c - lse_c) * 0.5
+    cvec[3] = lse_c
+    cvec[1] = pot_c
+    row_lse(3)
+    lse_r = take_rows(1)
+    pot_r = (pot_r - lse_r) * 0.5
+    to_rows(pot_r, rvec.at[1])
+    col_lse(3)
+    to_rows(lse_r, rvec.at[3])
 
     first_col = (lax.broadcasted_iota(jnp.int32, (8, BLOCK), 1) + b * BLOCK).astype(F32)
     first_col = jnp.broadcast_to(first_col[0:1], (CH, BLOCK))
@@ -390,43 +437,38 @@
         lax.fori_loop(0, count, step, 0)
 
     def col_sums(e, sums):
-        cmsg[e, 0:PLANE, :] = jnp.concatenate([jnp.sum(v, axis=0, keepdims=True) for v in sums], axis=0)
+        cmsg[e] = jnp.concatenate([jnp.sum(v, axis=0, keepdims=True) for v in sums], axis=0)
         send_cols(e)
 
-    wait_rows(2)
-    lse_r = merge(rrx[2, :, 0:LINE, :])
-    to_rows(lse_r, rvec.at[4])
+    to_rows(take_rows(2), rvec.at[4])
     sums, picked = add_term(3)
-    cmsg[3, PLANE : PLANE + 8, :] = picked
     col_sums(3, sums)
-    wait_cols(2)
-    lse_c = merge(crx[2, :, 0:PLANE, :])
+    lse_c = take_cols(2)
     cvec[4] = lse_c
     pot_c = (pot_c - lse_c) * 0.5
     add_mirror(3)
     rmsg[3, 0:LINE, :] = row_sums(accr)
+    rmsg[3, LINE : LINE + 8, :] = picked + (2.0 / PLANE) * (pot_c[0:8] + pot_c[8:16])
     send_rows(3)
+    wait_cols(3)
+    cot_c = -1.0 + jnp.sum(crx[3], axis=0)
+    cvec[5] = -0.5 * cot_c
+    add_mirror(2)
+    rmsg[4, 0:LINE, :] = row_sums(accr)
+    send_rows(4)
     wait_rows(3)
     cot_r = -1.0 + jnp.sum(rrx[3, :, 0:LINE, :], axis=0)
     to_rows(-0.5 * cot_r, rvec.at[5])
     sums, _ = add_term(2)
     col_sums(4, sums)
-    wait_cols(3)
-    cot_c = -1.0 + jnp.sum(crx[3, :, 0:PLANE, :], axis=0)
-    cvec[5] = -0.5 * cot_c
-    picked = jnp.sum(crx[3, :, PLANE : PLANE + 8, :], axis=0)
-    rmsg[4, LINE : LINE + 8, :] = picked + 2.0 * (pot_c[0:8] + pot_c[8:16])
-    add_mirror(2)
-    rmsg[4, 0:LINE, :] = row_sums(accr)
-    send_rows(4)
+    lmsg[...] = jnp.sum(rrx[3, :, LINE : LINE + 8, :], axis=0)
+    send_loss()
     wait_rows(4)
     cot_r = 0.5 * cot_r + jnp.sum(rrx[4, :, 0:LINE, :], axis=0)
-    whole = jnp.sum(rrx[4, :, LINE : LINE + 8, :], axis=0)
-    loss[0, 0] = jnp.sum(whole) * (-LN2 / TOTAL)
     to_rows(-0.5 * cot_r, rvec.at[6])
     add_term(1)
     wait_cols(4)
-    cot_c = 0.5 * cot_c + jnp.sum(crx[4, :, 0:PLANE, :], axis=0)
+    cot_c = 0.5 * cot_c + jnp.sum(crx[4], axis=0)
     cvec[6] = -0.5 * cot_c
 
     grad_scale = 1.0 / math.sqrt(WIDTH)
@@ -499,6 +541,11 @@
     finish(2)
     finish(3)
 
+    every = lrx.at[pl.ds(0, PLANE - 1)]
+    pltpu.make_async_copy(every, every, losem.at[1]).wait()
+    loss[0, 0] = jnp.sum(lrx[...]) * (-LN2 / TOTAL)
+
+    pltpu.make_async_copy(every, every, losem.at[0]).wait()
     sent = ec.at[pl.ds(0, PLANE - 1)]
     pltpu.make_async_copy(sent, sent, psend).wait()
     sent = er.at[pl.ds(0, LINE - 1)]
@@ -536,10 +583,12 @@
             vec((RROWS, BLOCK), F32),
             vec((RROWS, BLOCK), F32),
             vec((RROWS, BLOCK), F32),
-            vec((5, PLANE + 8, BLOCK), F32),
-            vec((5, PLANE, PLANE + 8, BLOCK), F32),
+            vec((5, PLANE, BLOCK), F32),
+            vec((5, PLANE, PLANE, BLOCK), F32),
             vec((5, LINE + 8, BLOCK), F32),
             vec((5, LINE, LINE + 8, BLOCK), F32),
+            vec((8, BLOCK), F32),
+            vec((PLANE, 8, BLOCK), F32),
             vec((SIDE, 2, SIDE, BLOCK, TILE), F32),
             vec((SIDE, SIDE, BLOCK, TILE), F32),
             vec((SIDE, 2, BLOCK, TILE // 2), BF16),
@@ -555,6 +604,7 @@
             dma((5,)),
             dma((5,)),
             dma((5,)),
+            dma((2,)),
             dma((SIDE,)),
             dma((SIDE,)),
             dma((16,)),

time: 102 us -> 96.3 us (0.944)
  Pallas kernels: 97.4 us -> 91.6 us
    pallas_call x1, Pallas kernels: 97.4 us -> 91.6 us  [shards(): pl.pallas_call(kernel, out_shape=(jax.ShapeDtypeStruct((BLOCK, WIDTH), F3...]
where the time goes in v4:
time: 96.3 us; the launch traced here: 95.9 us
  Pallas kernels  91.6 us (95%)
  between operations  2.33 us (2%)
  local copies, waits for them, and re-layouts  1.89 us (2%)
    pallas_call x1, Pallas kernels, shards(): pl.pallas_call(kernel, out_shape=(jax.ShapeDtypeStruct((BLOCK, WIDTH), F3...  91.6 us

profile of v4, /device:TPU:1, one launch (start us, length us, event | category | flops | bytes accessed | tf_op | source)
XLA Modules:
  0.0 95.9 jit_solution(10369748354679433651)
XLA Ops:
  0.6 91.6 %shard_map.41 = (f32[128,1024]{1,0:T(8,128)}, f32[1,1]{1,0:T(1,128)}) custom-call(bf16[128,1024]{1,0:T(8,128)(2,1)} %emb.1, s32[1,128]{1,0:T(1,128)} %bitcast.2), custom_call_target="tpu_custom_call" | custom-call | tf_op jit(solution)/shard_map/pallas_call | solution.py:567
  92.8 1.9 %copy.7 = f32[128,1024]{1,0:T(8,128)} copy(f32[128,1024]{1,0:T(8,128)} %get-tuple-element.9) | data formatting | bytes 1048576

commit v5 on v4

--- a/solution.py
+++ b/solution.py
@@ -22,7 +22,7 @@
 F32 = jnp.float32
 BF16 = jnp.bfloat16
 TILE = 256
-SCORE_M = 4
+SCORE_M = 8
 CH = 64
 OFFS = (0, -1, 1, 2)
 FAR_FIRST = sorted(
@@ -45,9 +45,9 @@
 
 
 def kernel(
-    emb, pos, grad, loss,
-    ec, er, s, w, wb, rvec, cvec, pr_ref, mr, accr, cmsg, crx, rmsg, rrx,
-    lmsg, lrx, gp, rb, xs2, xr2, xs1, xr1,
+    emb, pos, own, parts, loss,
+    ec, er, s, w, wb, kept, term2, rvec, cvec, pr_ref, mr, accr, cmsg, crx, rmsg, rrx,
+    lmsg, lrx, gp, rb, xs, xr,
     lsem, psend, prsem, xsend, xrsem, csend, crecv, rsend, rrecv, losem, gsend, grecv, hsend, hrecv,
 ):
     me = lax.axis_index("dp")
@@ -164,40 +164,24 @@
 
     score_scale = LOG2E / math.sqrt(WIDTH)
 
-    def score_tile(dy, other):
-        half = z // 2
-        n = lax.rem(y + dy + SIDE, SIDE) * 2 + (1 - half if other else half)
+    def score_tile(n):
         right = ec[pl.ds(2 * n, 2)].reshape(2 * BLOCK, WIDTH)
         cols = pl.ds(pl.multiple_of(n * 256, 256), 256)
-
-        def part(m, carry):
+        for m in range(LINE // SCORE_M):
             left = er[pl.ds(SCORE_M * m, SCORE_M)].reshape(SCORE_M * BLOCK, WIDTH)
             out = lax.dot_general(left, right, (((1,), (1,)), ((), ())), preferred_element_type=F32)
-            s[pl.ds(pl.multiple_of(m * (SCORE_M * BLOCK), SCORE_M * BLOCK), SCORE_M * BLOCK), cols] = out * score_scale
-            return carry
-
-        lax.fori_loop(0, LINE // SCORE_M, part, 0)
-        if dy == 0 and not other:
-            dr = pl.ds(pl.multiple_of(b * BLOCK, BLOCK), BLOCK)
-            dc = pl.ds(pl.multiple_of(a * BLOCK, BLOCK), BLOCK)
-            s[dr, dc] = jnp.where(eye, -30000.0 * LOG2E, s[dr, dc])
-        first_sums(n, dy == 0 and not other)
-
-    def first_sums(n, fresh):
+            s[pl.ds(m * SCORE_M * BLOCK, SCORE_M * BLOCK), cols] = out * score_scale
+
+    def first_sums(n):
         two = [pl.ds(pl.multiple_of(n * 256 + k * BLOCK, BLOCK), BLOCK) for k in range(2)]
 
         def step(i, carry):
             rows = rows_at(i)
             v = [s[rows, c] for c in two]
-            top = jnp.maximum(v[0], v[1])
-            if not fresh:
-                old = mr[rows, :]
-                top = jnp.maximum(top, old)
-            acc = jnp.exp2(v[0] - top) + jnp.exp2(v[1] - top)
-            if not fresh:
-                acc = acc + accr[rows, :] * jnp.exp2(old - top)
+            old = mr[rows, :]
+            top = jnp.maximum(jnp.maximum(v[0], v[1]), old)
             mr[rows, :] = top
-            accr[rows, :] = acc
+            accr[rows, :] = accr[rows, :] * jnp.exp2(old - top) + (jnp.exp2(v[0] - top) + jnp.exp2(v[1] - top))
             out = []
             for k in range(2):
                 old, acc = carry[k]
@@ -224,25 +208,57 @@
             wait_plane(h, o, 1, 0, 64, 5 + 4 * oi)
             send_plane(h, o, 1, 32, 32, 0, -1, 7 + 4 * oi)
 
-    score_tile(0, False)
-    second_stage(1)
-    wait_forwarded(1, 0)
-    score_tile(0, True)
-    second_stage(2)
-    score_tile(-1, False)
-    score_tile(1, False)
-    second_stage(3)
-    wait_forwarded(1, 1)
-    wait_forwarded(1, 2)
-    score_tile(-1, True)
-    score_tile(1, True)
-    wait_forwarded(0, 0)
-    wait_forwarded(0, 1)
-    wait_forwarded(0, 2)
-    score_tile(2, False)
-    wait_forwarded(0, 3)
-    wait_forwarded(1, 3)
-    score_tile(2, True)
+    def tile_step(i, carry):
+        @pl.when(i == 1)
+        def _():
+            second_stage(1)
+            wait_forwarded(1, 0)
+
+        @pl.when(i == 2)
+        def _():
+            second_stage(2)
+
+        @pl.when(i == 4)
+        def _():
+            second_stage(3)
+            wait_forwarded(1, 1)
+            wait_forwarded(1, 2)
+
+        @pl.when(i == 6)
+        def _():
+            wait_forwarded(0, 0)
+            wait_forwarded(0, 1)
+            wait_forwarded(0, 2)
+
+        @pl.when(i == 7)
+        def _():
+            wait_forwarded(0, 3)
+            wait_forwarded(1, 3)
+
+        def pick(values):
+            out = values[0]
+            for k in range(1, 8):
+                out = jnp.where(i == k, values[k], out)
+            return out
+
+        half = z // 2
+        other = pick((0, 1, 0, 0, 1, 1, 0, 1))
+        n = lax.rem(y + pick((0, 0, 3, 1, 3, 1, 2, 2)), SIDE) * 2 + lax.rem(half + other, 2)
+        score_tile(n)
+
+        @pl.when(i == 0)
+        def _():
+            dr = pl.ds(pl.multiple_of(b * BLOCK, BLOCK), BLOCK)
+            dc = pl.ds(pl.multiple_of(a * BLOCK, BLOCK), BLOCK)
+            s[dr, dc] = jnp.where(eye, -30000.0 * LOG2E, s[dr, dc])
+
+        first_sums(n)
+        return carry
+
+    mr[...] = jnp.full((RROWS, BLOCK), -3e38, F32)
+    accr[...] = jnp.zeros((RROWS, BLOCK), F32)
+    lax.fori_loop(0, 8, tile_step, 0)
+
     def lanes(k):
         return slice(k * BLOCK, (k + 1) * BLOCK)
 
@@ -262,10 +278,14 @@
             ).start()
         crx[e, a] = cmsg[e]
 
+    def row_part(e):
+        return pl.ds(0, LINE + 8 if e in (0, 3) else LINE)
+
     def send_rows(e):
         for dx, other in ((2, 1), (2, 0), (1, 1), (-1, 1), (1, 0), (-1, 0), (0, 1)):
             pltpu.make_async_remote_copy(
-                src_ref=rmsg.at[e], dst_ref=rrx.at[e, b], send_sem=rsend.at[e], recv_sem=rrecv.at[e],
+                src_ref=rmsg.at[e, row_part(e)], dst_ref=rrx.at[e, b, row_part(e)],
+                send_sem=rsend.at[e], recv_sem=rrecv.at[e],
                 device_id=(dev_of(0, 0, dx, 1 - core if other else core),), device_id_type=MESH,
             ).start()
         rrx[e, b] = rmsg[e]
@@ -275,7 +295,7 @@
         pltpu.make_async_copy(every, every, crecv.at[e]).wait()
 
     def wait_rows(e):
-        every = rrx.at[e, pl.ds(0, LINE - 1)]
+        every = rrx.at[e, pl.ds(0, LINE - 1), row_part(e)]
         pltpu.make_async_copy(every, every, rrecv.at[e]).wait()
 
     def send_loss():
@@ -335,9 +355,13 @@
         def sum_step(i, sums):
             rows = rows_at(i)
             pr = pot_r[rows, :]
-            return tuple(
-                sums[k] + fold(jnp.exp2(value(rows, k, pr) - cvec[7, k : k + 1, :]), jnp.add) for k in range(PLANE)
-            )
+            out = []
+            for k in range(PLANE):
+                p = jnp.exp2(value(rows, k, pr) - cvec[7, k : k + 1, :])
+                if t == 3:
+                    kept[rows, lanes(k)] = p
+                out.append(sums[k] + fold(p, jnp.add))
+            return tuple(out)
 
         sums = lax.fori_loop(0, steps, sum_step, (zero,) * PLANE)
         csum = jnp.concatenate([jnp.sum(v, axis=0, keepdims=True) for v in sums], axis=0)
@@ -382,56 +406,82 @@
     first_col = jnp.broadcast_to(first_col[0:1], (CH, BLOCK))
 
     def add_term(t):
-        pot_cc, lse_rr, pull_rr = cvec.at[t - 2], rvec.at[t + 1], rvec.at[7 - t]
-
         def step(i, carry):
             sums, picked = carry
             rows = rows_at(i)
-            lr = lse_rr[rows, :]
             if t < 3:
-                qr = pull_rr[rows, :]
+                qr = rvec[5, rows, :]
             else:
+                lr = rvec[4, rows, :]
                 partner = pr_ref[rows, :] - first_col
             out = []
             for k in range(PLANE):
-                v = s[rows, lanes(k)]
-                u = v + pot_cc[k : k + 1, :] if t > 1 else v
-                term = jnp.exp2(u - lr)
                 if t < 3:
-                    term = term * qr
+                    term = term2[rows, lanes(k)] * qr
                     w[rows, lanes(k)] = w[rows, lanes(k)] + term
                 else:
+                    v = s[rows, lanes(k)]
+                    term = jnp.exp2(v + cvec[1, k : k + 1, :] - lr)
                     hit = partner == float(k * RROWS)
                     picked = picked + fold(jnp.where(hit, v, 0.0), jnp.add)
                     w[rows, lanes(k)] = jnp.where(hit, term - 2.0, term)
-                if t > 1:
-                    out.append(sums[k] + fold(term, jnp.add))
+                out.append(sums[k] + fold(term, jnp.add))
             return tuple(out), picked
 
-        return lax.fori_loop(0, steps, step, ((zero,) * (PLANE if t > 1 else 0), zero))
-
-    def add_mirror(t, start=0, count=steps):
-        pot_rr, lse_cc, pull_cc = rvec.at[t - 2], cvec.at[t + 1], cvec.at[7 - t]
-
+        return lax.fori_loop(0, steps, step, ((zero,) * PLANE, zero))
+
+    def add_mirror(factor):
+        def step(i, carry):
+            rows = rows_at(i)
+            acc = None
+            for k in range(PLANE):
+                mirror = kept[rows, lanes(k)] * factor[k : k + 1, :]
+                w[rows, lanes(k)] = w[rows, lanes(k)] + mirror
+                acc = mirror if acc is None else acc + mirror
+            accr[rows, :] = acc
+            return carry
+
+        lax.fori_loop(0, steps, step, 0)
+
+    def keep_term():
+        def step(i, carry):
+            rows = rows_at(i)
+            lr = rvec[3, rows, :]
+            for k in range(PLANE):
+                term2[rows, lanes(k)] = jnp.exp2(s[rows, lanes(k)] + cvec[0, k : k + 1, :] - lr)
+            return carry
+
+        lax.fori_loop(0, steps, step, 0)
+
+    def keep_mirror(t):
+        def step(i, carry):
+            rows = rows_at(i)
+            for k in range(PLANE):
+                v = s[rows, lanes(k)]
+                if t == 2:
+                    v = v + rvec[0, rows, :]
+                kept[rows, lanes(k)] = jnp.exp2(v - cvec[t + 1, k : k + 1, :])
+            return carry
+
+        lax.fori_loop(0, steps, step, 0)
+
+    def add_first_term():
+        def step(i, carry):
+            rows = rows_at(i)
+            lr = rvec[2, rows, :]
+            qr = rvec[6, rows, :]
+            for k in range(PLANE):
+                w[rows, lanes(k)] = w[rows, lanes(k)] + jnp.exp2(s[rows, lanes(k)] - lr) * qr
+            return carry
+
+        lax.fori_loop(0, steps, step, 0)
+
+    def round_weights(start, count):
         def step(i, carry):
             rows = rows_at(start + i)
-            if t > 1:
-                pr = pot_rr[rows, :]
-            acc = None
             for k in range(PLANE):
-                v = s[rows, lanes(k)]
-                q = v + pr if t > 1 else v
-                mirror = jnp.exp2(q - lse_cc[k : k + 1, :])
-                if t < 3:
-                    mirror = mirror * pull_cc[k : k + 1, :]
-                total = w[rows, lanes(k)] + mirror
-                if t > 1:
-                    w[rows, lanes(k)] = total
-                    acc = mirror if acc is None else acc + mirror
-                else:
-                    wb[rows, lanes(k)] = total.astype(BF16)
-            if t > 1:
-                accr[rows, :] = acc
+                total = w[rows, lanes(k)] + kept[rows, lanes(k)] * cvec[6, k : k + 1, :]
+                wb[rows, lanes(k)] = total.astype(BF16)
             return carry
 
         lax.fori_loop(0, count, step, 0)
@@ -443,17 +493,19 @@
     to_rows(take_rows(2), rvec.at[4])
     sums, picked = add_term(3)
     col_sums(3, sums)
+    keep_term()
     lse_c = take_cols(2)
-    cvec[4] = lse_c
     pot_c = (pot_c - lse_c) * 0.5
-    add_mirror(3)
+    cvec[4] = jnp.exp2(cvec[7] - lse_c)
+    add_mirror(cvec.at[4])
     rmsg[3, 0:LINE, :] = row_sums(accr)
     rmsg[3, LINE : LINE + 8, :] = picked + (2.0 / PLANE) * (pot_c[0:8] + pot_c[8:16])
     send_rows(3)
+    keep_mirror(2)
     wait_cols(3)
     cot_c = -1.0 + jnp.sum(crx[3], axis=0)
     cvec[5] = -0.5 * cot_c
-    add_mirror(2)
+    add_mirror(cvec.at[5])
     rmsg[4, 0:LINE, :] = row_sums(accr)
     send_rows(4)
     wait_rows(3)
@@ -463,83 +515,85 @@
     col_sums(4, sums)
     lmsg[...] = jnp.sum(rrx[3, :, LINE : LINE + 8, :], axis=0)
     send_loss()
+    keep_mirror(1)
     wait_rows(4)
     cot_r = 0.5 * cot_r + jnp.sum(rrx[4, :, 0:LINE, :], axis=0)
     to_rows(-0.5 * cot_r, rvec.at[6])
-    add_term(1)
+    add_first_term()
     wait_cols(4)
     cot_c = 0.5 * cot_c + jnp.sum(crx[4], axis=0)
     cvec[6] = -0.5 * cot_c
 
     grad_scale = 1.0 / math.sqrt(WIDTH)
 
-    add_mirror(1)
-
-    def product(n):
-        right = ec[:, :, pl.ds(n * TILE, TILE)].reshape(CCOLS, TILE)
-        for m in range(2):
-            out = jnp.dot(wb[pl.ds(m * 512, 512), :], right, preferred_element_type=F32) * grad_scale
-            for g in range(4):
-                block = 4 * m + g
-                gp[n, block % 2, block // 2] = out[g * BLOCK : (g + 1) * BLOCK]
+    def product(d):
+        xx = lax.rem(x + d, SIDE)
+        round_weights(xx * (2 * BLOCK // CH), 2 * BLOCK // CH)
+        rows = pl.ds(pl.multiple_of(xx * 2 * BLOCK, 2 * BLOCK), 2 * BLOCK)
+        left = wb[rows, :]
+        for n in range(WIDTH // TILE):
+            right = ec[:, :, pl.ds(n * TILE, TILE)].reshape(CCOLS, TILE)
+            out = jnp.dot(left, right, preferred_element_type=F32) * grad_scale
+            gp[d, :, :, n * TILE : (n + 1) * TILE] = out.reshape(2, BLOCK, TILE)
         pltpu.make_async_remote_copy(
-            src_ref=gp.at[n, 1 - core], dst_ref=rb.at[n], send_sem=gsend.at[n], recv_sem=grecv.at[n],
+            src_ref=gp.at[d, 1 - core], dst_ref=rb.at[d], send_sem=gsend.at[d], recv_sem=grecv.at[d],
             device_id=(sibling,), device_id_type=MESH,
         ).start()
 
-    def ring(src, dst, i, dx):
+    def chip_sum(d):
+        pltpu.make_async_copy(rb.at[d], rb.at[d], grecv.at[d]).wait()
+        return gp[d, core] + rb[d]
+
+    def ring(n, i, dx):
         return pltpu.make_async_remote_copy(
-            src_ref=src, dst_ref=dst, send_sem=hsend.at[i], recv_sem=hrecv.at[i],
+            src_ref=xs.at[n, i], dst_ref=xr.at[i] if n == 0 else parts.at[n - 1, i],
+            send_sem=hsend.at[2 * n + i], recv_sem=hrecv.at[2 * n + i],
             device_id=(xdev(dx),), device_id_type=MESH,
         )
 
-    half = TILE // 2
-    first = [[ring(xs1.at[n, i], xr1.at[n, i], 4 * n + i, dx) for i, dx in ((0, 1), (1, -1))] for n in range(SIDE)]
-    second = [[ring(xs2.at[n, i], xr2.at[n, i], 4 * n + 2 + i, dx) for i, dx in ((0, 1), (1, -1))] for n in range(SIDE)]
-
-    def chip_sum(n, d):
-        xx = lax.rem(x + d, SIDE)
-        return gp[n, core, xx] + rb[n, xx]
-
-    def send_first(n):
-        pltpu.make_async_copy(rb.at[n], rb.at[n], grecv.at[n]).wait()
-        far = chip_sum(n, 2).astype(BF16)
-        xs1[n, 0, :, :half] = far[:, :half]
-        xs1[n, 0, :, half:] = chip_sum(n, 1)[:, half:].astype(BF16)
-        first[n][0].start()
-        xs1[n, 1, :, half:] = far[:, half:]
-        xs1[n, 1, :, :half] = chip_sum(n, 3)[:, :half].astype(BF16)
-        first[n][1].start()
-
-    def send_second(n):
-        first[n][0].wait_recv()
-        xs2[n, 0] = (chip_sum(n, 1)[:, :half] + xr1[n, 0, :, :half].astype(F32)).astype(BF16)
-        second[n][0].start()
-        first[n][1].wait_recv()
-        xs2[n, 1] = (chip_sum(n, 3)[:, half:] + xr1[n, 1, :, half:].astype(F32)).astype(BF16)
-        second[n][1].start()
-
-    def finish(n):
-        own = chip_sum(n, 0)
-        second[n][0].wait_recv()
-        second[n][1].wait_recv()
-        lo, mid = n * TILE, n * TILE + half
-        grad[:, lo:mid] = own[:, :half] + xr2[n, 0].astype(F32) + xr1[n, 1, :, :half].astype(F32)
-        grad[:, mid : mid + half] = own[:, half:] + xr2[n, 1].astype(F32) + xr1[n, 0, :, half:].astype(F32)
-
-    for n in range(SIDE):
-        product(n)
-        if n >= 1:
-            send_first(n - 1)
-        if n >= 2:
-            send_second(n - 2)
-    send_first(3)
-    send_second(2)
-    finish(0)
-    finish(1)
-    send_second(3)
-    finish(2)
-    finish(3)
+    half = WIDTH // 2
+    far, direct, near = [[ring(n, i, dx) for i, dx in ((0, 1), (1, -1))] for n in range(3)]
+
+    def product_step(i, carry):
+        product(jnp.where(i == 0, 2, jnp.where(i == 1, 1, jnp.where(i == 2, 3, 0))))
+
+        @pl.when(i == 1)
+        def _():
+            v = chip_sum(2).astype(BF16)
+            xs[0, 0] = v[:, :half]
+            far[0].start()
+            xs[0, 1] = v[:, half:]
+            far[1].start()
+
+        @pl.when(i == 2)
+        def _():
+            v = chip_sum(1)
+            xs[1, 0] = v[:, half:].astype(BF16)
+            direct[0].start()
+            rb[1, :, :half] = v[:, :half]
+
+        @pl.when(i == 3)
+        def _():
+            v = chip_sum(3)
+            xs[1, 1] = v[:, :half].astype(BF16)
+            direct[1].start()
+            rb[3, :, half:] = v[:, half:]
+
+        return carry
+
+    lax.fori_loop(0, SIDE, product_step, 0)
+    far[0].wait_recv()
+    xs[2, 0] = (rb[1, :, :half] + xr[0].astype(F32)).astype(BF16)
+    near[0].start()
+    far[1].wait_recv()
+    xs[2, 1] = (rb[3, :, half:] + xr[1].astype(F32)).astype(BF16)
+    near[1].start()
+    rb[0] = chip_sum(0)
+    result = pltpu.make_async_copy(rb.at[0], own, lsem.at[2])
+    result.start()
+    for c in direct + near:
+        c.wait_recv()
+    result.wait()
 
     every = lrx.at[pl.ds(0, PLANE - 1)]
     pltpu.make_async_copy(every, every, losem.at[1]).wait()
@@ -551,33 +605,47 @@
     sent = er.at[pl.ds(0, LINE - 1)]
     pltpu.make_async_copy(sent, sent, xsend).wait()
     for e in range(5):
-        every = rrx.at[e, pl.ds(0, LINE - 1)]
+        every = rrx.at[e, pl.ds(0, LINE - 1), row_part(e)]
         pltpu.make_async_copy(every, every, rsend.at[e]).wait()
         every = crx.at[e, pl.ds(0, PLANE - 1)]
         pltpu.make_async_copy(every, every, csend.at[e]).wait()
     for d in range(SIDE):
         pltpu.make_async_copy(rb.at[d], rb.at[d], gsend.at[d]).wait()
-    for c in sum(first + second, []):
+    for c in far + direct + near:
         c.wait_send()
+
+
+def add_parts(own, parts, total, grad, loss):
+    half = WIDTH // 2
+    grad[:, :half] = own[:, :half] + parts[0, 1].astype(F32) + parts[1, 0].astype(F32)
+    grad[:, half:] = own[:, half:] + parts[0, 0].astype(F32) + parts[1, 1].astype(F32)
+    loss[0, 0] = total[0, 0]
 
 
 def shards(embeddings, positives):
     vec = pltpu.VMEM
     dma = pltpu.SemaphoreType.DMA
-    grad, loss = pl.pallas_call(
+    own, parts, total = pl.pallas_call(
         kernel,
         out_shape=(
             jax.ShapeDtypeStruct((BLOCK, WIDTH), F32),
+            jax.ShapeDtypeStruct((2, 2, BLOCK, WIDTH // 2), BF16),
             jax.ShapeDtypeStruct((1, 1), F32),
         ),
         in_specs=[pl.BlockSpec(memory_space=pl.ANY), pl.BlockSpec(memory_space=pltpu.VMEM)],
-        out_specs=(pl.BlockSpec(memory_space=pltpu.VMEM), pl.BlockSpec(memory_space=pltpu.SMEM)),
+        out_specs=(
+            pl.BlockSpec(memory_space=pl.ANY),
+            pl.BlockSpec(memory_space=pl.ANY),
+            pl.BlockSpec(memory_space=pltpu.SMEM),
+        ),
         scratch_shapes=[
             vec((PLANE, BLOCK, WIDTH), BF16),
             vec((LINE, BLOCK, WIDTH), BF16),
             vec((RROWS, CCOLS), F32),
             vec((RROWS, CCOLS), F32),
             vec((RROWS, CCOLS), BF16),
+            vec((RROWS, CCOLS), F32),
+            vec((RROWS, CCOLS), F32),
             vec((7, RROWS, BLOCK), F32),
             vec((8, PLANE, BLOCK), F32),
             vec((RROWS, BLOCK), F32),
@@ -589,13 +657,11 @@
             vec((5, LINE, LINE + 8, BLOCK), F32),
             vec((8, BLOCK), F32),
             vec((PLANE, 8, BLOCK), F32),
-            vec((SIDE, 2, SIDE, BLOCK, TILE), F32),
-            vec((SIDE, SIDE, BLOCK, TILE), F32),
-            vec((SIDE, 2, BLOCK, TILE // 2), BF16),
-            vec((SIDE, 2, BLOCK, TILE // 2), BF16),
-            vec((SIDE, 2, BLOCK, TILE), BF16),
-            vec((SIDE, 2, BLOCK, TILE), BF16),
-            dma((2,)),
+            vec((SIDE, 2, BLOCK, WIDTH), F32),
+            vec((SIDE, BLOCK, WIDTH), F32),
+            vec((3, 2, BLOCK, WIDTH // 2), BF16),
+            vec((2, BLOCK, WIDTH // 2), BF16),
+            dma((3,)),
             dma,
             dma((2, 20)),
             dma,
@@ -607,13 +673,24 @@
             dma((2,)),
             dma((SIDE,)),
             dma((SIDE,)),
-            dma((16,)),
-            dma((16,)),
+            dma((6,)),
+            dma((6,)),
         ],
         compiler_params=pltpu.CompilerParams(
-            collective_id=0, has_side_effects=True, vmem_limit_bytes=56 * 1024 * 1024
+            collective_id=0, has_side_effects=True, vmem_limit_bytes=60 * 1024 * 1024
         ),
     )(embeddings, positives.reshape(1, BLOCK))
+    grad, loss = pl.pallas_call(
+        add_parts,
+        out_shape=(jax.ShapeDtypeStruct((BLOCK, WIDTH), F32), jax.ShapeDtypeStruct((1, 1), F32)),
+        grid=(2,),
+        in_specs=[
+            pl.BlockSpec((BLOCK // 2, WIDTH), lambda i: (i, 0)),
+            pl.BlockSpec((2, 2, BLOCK // 2, WIDTH // 2), lambda i: (0, 0, i, 0)),
+            pl.BlockSpec(memory_space=pltpu.SMEM),
+        ],
+        out_specs=(pl.BlockSpec((BLOCK // 2, WIDTH), lambda i: (i, 0)), pl.BlockSpec(memory_space=pltpu.SMEM)),
+    )(own, parts, total)
     return loss.reshape(()), grad
 
 

time: 96.3 us -> 89.3 us (0.927)
  Pallas kernels: 91.6 us -> 88.5 us
  local copies, waits for them, and re-layouts: 1.89 us -> 0 us
  between operations: 2.33 us -> 0.64 us
    pallas_call x1, Pallas kernels: 91.6 us -> 86 us  [shards(): pl.pallas_call(kernel, out_shape=(jax.ShapeDtypeStruct((BLOCK, WIDTH), F3...]
    pallas_call x0 -> x1, Pallas kernels: none -> 2.58 us  [shards(): pl.pallas_call(add_parts, out_shape=(jax.ShapeDtypeStruct((BLOCK, WIDTH),...]
    unnamed x1 -> x0, local copies, waits for them, and re-layouts: 1.89 us -> none
where the time goes in v5:
time: 89.3 us; the launch traced here: 89.2 us
  Pallas kernels  88.5 us (99%)
    pallas_call x1, Pallas kernels, shards(): pl.pallas_call(kernel, out_shape=(jax.ShapeDtypeStruct((BLOCK, WIDTH), F3...  86 us
    pallas_call x1, Pallas kernels, shards(): pl.pallas_call(add_parts, out_shape=(jax.ShapeDtypeStruct((BLOCK, WIDTH),...  2.58 us

profile of v5, /device:TPU:1, one launch (start us, length us, event | category | flops | bytes accessed | tf_op | source)
XLA Modules:
  0.0 89.2 jit_solution(3901045955354900887)
XLA Ops:
  0.6 86.0 %shard_map.41 = (f32[128,1024]{1,0:T(8,128)}, bf16[2,2,128,512]{3,2,1,0:T(8,128)(2,1)}, f32[1,1]{1,0:T(1,128)}) custom-call(bf16[128,1024]{1,0:T(8,128)(2,1)} %emb.1, s32[1,128]{1,0:T(1,128)} %bitcast.2), custom_call_target="tpu_custom_call" | custom-call | tf_op jit(solution)/shard_map/pallas_call | solution.py:628
  86.6 2.6 %shard_map.42 = (f32[128,1024]{1,0:T(8,128)}, f32[1,1]{1,0:T(1,128)}) custom-call(f32[128,1024]{1,0:T(8,128)} %get-tuple-element.7.own, bf16[2,2,128,512]{3,2,1,0:T(8,128)(2,1)} %get-tuple-element.8.parts, f32[1,1]{1,0:T(1,128)} %get-tuple-element.9.total), custom_call_target="tpu_custom_call" | custom-call | tf_op jit(solution)/shard_map/pallas_call | solution.py:683

commit v6 on v5

--- a/solution.py
+++ b/solution.py
@@ -25,6 +25,8 @@
 SCORE_M = 8
 CH = 64
 OFFS = (0, -1, 1, 2)
+OWN_SLOTS = (1, 4, 5, 6)
+FORWARD_SLOTS = (3, 7, 8, 9)
 FAR_FIRST = sorted(
     ((dy, dz) for dy in OFFS for dz in OFFS if (dy, dz) != (0, 0)), key=lambda d: -abs(d[0]) - abs(d[1])
 )
@@ -78,12 +80,12 @@
         dy, dz = (oq, op) if h == 0 else (op, oq)
         return lax.rem(y + dy + SIDE, SIDE) * SIDE + lax.rem(z + dz + SIDE, SIDE)
 
-    def send_plane(h, op, oq, lo, n, tp, tq, idx):
+    def send_plane(h, op, oq, lo, n, tp, tq, idx, slot):
         k = blk(h, op, oq)
         rows = pl.ds(64 * h + lo, n)
         src = emb.at[rows] if (op, oq) == (0, 0) else ec.at[k, rows]
         pltpu.make_async_remote_copy(
-            src_ref=src, dst_ref=ec.at[k, rows], send_sem=psend, recv_sem=prsem.at[h, idx],
+            src_ref=src, dst_ref=ec.at[k, rows], send_sem=psend.at[slot], recv_sem=prsem.at[h, idx],
             device_id=(blk(h, tp, tq) * LINE + b,), device_id_type=MESH,
         ).start()
 
@@ -112,40 +114,66 @@
         ref = er.at[k, pl.ds(lo, n)]
         pltpu.make_async_copy(ref, ref, xrsem.at[idx]).wait()
 
-    for h in (0, 1):
-        send_plane(h, 0, 0, 0, 64, 1, 0, 0)
-        send_plane(h, 0, 0, 0, 64, -1, 0, 1)
+    def issue(slot):
+        for h in (0, 1):
+            if slot == 0:
+                send_plane(h, 0, 0, 0, 64, 1, 0, 0, slot)
+                send_plane(h, 0, 0, 0, 64, -1, 0, 1, slot)
+            elif slot == 2:
+                send_plane(h, -1, 0, 0, 32, 1, 0, 2, slot)
+                send_plane(h, 1, 0, 32, 32, -1, 0, 3, slot)
+            elif slot in OWN_SLOTS:
+                oi = OWN_SLOTS.index(slot)
+                send_plane(h, OFFS[oi], 0, 0, 64, 0, 1, 4 + 4 * oi, slot)
+                send_plane(h, OFFS[oi], 0, 0, 64, 0, -1, 5 + 4 * oi, slot)
+            else:
+                oi = FORWARD_SLOTS.index(slot)
+                send_plane(h, OFFS[oi], -1, 0, 32, 0, 1, 6 + 4 * oi, slot)
+                send_plane(h, OFFS[oi], 1, 32, 32, 0, -1, 7 + 4 * oi, slot)
+
+    def sent(slot):
+        ref = ec.at[pl.ds(0, 1 if slot == 2 or slot in FORWARD_SLOTS else 2)]
+        pltpu.make_async_copy(ref, ref, psend.at[slot]).wait()
+
+    def arrived(slot):
+        for h in (0, 1):
+            if slot == 0:
+                wait_plane(h, -1, 0, 0, 64, 0)
+                wait_plane(h, 1, 0, 0, 64, 1)
+            elif slot == 2:
+                wait_plane(h, 2, 0, 0, 32, 2)
+                wait_plane(h, 2, 0, 32, 32, 3)
+            elif slot in OWN_SLOTS:
+                oi = OWN_SLOTS.index(slot)
+                wait_plane(h, OFFS[oi], -1, 0, 64, 4 + 4 * oi)
+                wait_plane(h, OFFS[oi], 1, 0, 64, 5 + 4 * oi)
+            else:
+                oi = FORWARD_SLOTS.index(slot)
+                wait_plane(h, OFFS[oi], 2, 0, 32, 6 + 4 * oi)
+                wait_plane(h, OFFS[oi], 2, 32, 32, 7 + 4 * oi)
+
+    issue(0)
     send_line(0, 0, 128, xdev(1), 0)
     send_line(0, 0, 128, xdev(-1), 1)
     send_line(0, 0, 128, sibling, 4)
-    for h in (0, 1):
-        send_plane(h, 0, 0, 0, 64, 0, 1, 4)
-        send_plane(h, 0, 0, 0, 64, 0, -1, 5)
-    for h in (0, 1):
-        wait_plane(h, -1, 0, 0, 64, 0)
-        send_plane(h, -1, 0, 0, 32, 1, 0, 2)
-        wait_plane(h, 1, 0, 0, 64, 1)
-        send_plane(h, 1, 0, 32, 32, -1, 0, 3)
+    issue(1)
+    arrived(0)
+    sent(0)
+    issue(2)
+    arrived(1)
+    sent(1)
+    issue(3)
     wait_line(xblk(-1), 0, 128, 0)
     send_line(-1, 0, 64, xdev(1), 2)
     send_line(-1, 0, 128, sibling, 5)
     wait_line(xblk(1), 0, 128, 1)
     send_line(1, 64, 64, xdev(-1), 3)
     send_line(1, 0, 128, sibling, 6)
-    for h in (0, 1):
-        for oi in (1, 2):
-            send_plane(h, OFFS[oi], 0, 0, 64, 0, 1, 4 + 4 * oi)
-            send_plane(h, OFFS[oi], 0, 0, 64, 0, -1, 5 + 4 * oi)
-    for h in (0, 1):
-        wait_plane(h, 0, -1, 0, 64, 4)
-        send_plane(h, 0, -1, 0, 32, 0, 1, 6)
-        wait_plane(h, 0, 1, 0, 64, 5)
-        send_plane(h, 0, 1, 32, 32, 0, -1, 7)
-    for h in (0, 1):
-        wait_plane(h, 2, 0, 0, 32, 2)
-        wait_plane(h, 2, 0, 32, 32, 3)
-        send_plane(h, 2, 0, 0, 64, 0, 1, 16)
-        send_plane(h, 2, 0, 0, 64, 0, -1, 17)
+    sent(2)
+    issue(4)
+    sent(3)
+    issue(5)
+    arrived(2)
     wait_line(xblk(2), 0, 64, 2)
     wait_line(xblk(2), 64, 64, 3)
     send_line(2, 0, 128, sibling, 7)
@@ -153,6 +181,8 @@
         wait_line(lax.rem(x + dx + SIDE, SIDE) * 2 + (1 - core), 0, 128, 4 + i)
     own_c.wait()
     own_r.wait()
+    sent(4)
+    issue(6)
 
     eye = lax.broadcasted_iota(jnp.int32, (BLOCK, BLOCK), 0) == lax.broadcasted_iota(jnp.int32, (BLOCK, BLOCK), 1)
     low = jnp.full((8, BLOCK), -3e38, F32)
@@ -196,44 +226,37 @@
             top = jnp.max(each, axis=0, keepdims=True)
             cmsg[0, pl.ds(2 * n + k, 1), :] = top + log2(jnp.sum(acc * jnp.exp2(each - top), axis=0, keepdims=True))
 
-    def wait_forwarded(h, oi):
-        wait_plane(h, OFFS[oi], 2, 0, 32, 6 + 4 * oi)
-        wait_plane(h, OFFS[oi], 2, 32, 32, 7 + 4 * oi)
-
-    def second_stage(oi):
-        o = OFFS[oi]
-        for h in (0, 1):
-            wait_plane(h, o, -1, 0, 64, 4 + 4 * oi)
-            send_plane(h, o, -1, 0, 32, 0, 1, 6 + 4 * oi)
-            wait_plane(h, o, 1, 0, 64, 5 + 4 * oi)
-            send_plane(h, o, 1, 32, 32, 0, -1, 7 + 4 * oi)
-
     def tile_step(i, carry):
         @pl.when(i == 1)
         def _():
-            second_stage(1)
-            wait_forwarded(1, 0)
+            arrived(3)
 
         @pl.when(i == 2)
         def _():
-            second_stage(2)
+            arrived(4)
+            sent(5)
+            issue(7)
+            arrived(5)
+
+        @pl.when(i == 3)
+        def _():
+            sent(6)
+            issue(8)
 
         @pl.when(i == 4)
         def _():
-            second_stage(3)
-            wait_forwarded(1, 1)
-            wait_forwarded(1, 2)
-
-        @pl.when(i == 6)
-        def _():
-            wait_forwarded(0, 0)
-            wait_forwarded(0, 1)
-            wait_forwarded(0, 2)
+            arrived(6)
+            sent(7)
+            issue(9)
+            arrived(7)
+
+        @pl.when(i == 5)
+        def _():
+            arrived(8)
 
         @pl.when(i == 7)
         def _():
-            wait_forwarded(0, 3)
-            wait_forwarded(1, 3)
+            arrived(9)
 
         def pick(values):
             out = values[0]
@@ -600,10 +623,10 @@
     loss[0, 0] = jnp.sum(lrx[...]) * (-LN2 / TOTAL)
 
     pltpu.make_async_copy(every, every, losem.at[0]).wait()
-    sent = ec.at[pl.ds(0, PLANE - 1)]
-    pltpu.make_async_copy(sent, sent, psend).wait()
-    sent = er.at[pl.ds(0, LINE - 1)]
-    pltpu.make_async_copy(sent, sent, xsend).wait()
+    sent(8)
+    sent(9)
+    every = er.at[pl.ds(0, LINE - 1)]
+    pltpu.make_async_copy(every, every, xsend).wait()
     for e in range(5):
         every = rrx.at[e, pl.ds(0, LINE - 1), row_part(e)]
         pltpu.make_async_copy(every, every, rsend.at[e]).wait()
@@ -662,7 +685,7 @@
             vec((3, 2, BLOCK, WIDTH // 2), BF16),
             vec((2, BLOCK, WIDTH // 2), BF16),
             dma((3,)),
-            dma,
+            dma((10,)),
             dma((2, 20)),
             dma,
             dma((8,)),

time: 89.3 us -> 87.3 us (0.978)
  Pallas kernels: 88.5 us -> 86.5 us
    pallas_call x1, Pallas kernels: 86 us -> 83.9 us  [shards(): pl.pallas_call(kernel, out_shape=(jax.ShapeDtypeStruct((BLOCK, WIDTH), F3...]
where the time goes in v6:
time: 87.3 us; the launch traced here: 87.2 us
  Pallas kernels  86.5 us (99%)
    pallas_call x1, Pallas kernels, shards(): pl.pallas_call(kernel, out_shape=(jax.ShapeDtypeStruct((BLOCK, WIDTH), F3...  83.9 us
    pallas_call x1, Pallas kernels, shards(): pl.pallas_call(add_parts, out_shape=(jax.ShapeDtypeStruct((BLOCK, WIDTH),...  2.58 us

profile of v6, /device:TPU:1, one launch (start us, length us, event | category | flops | bytes accessed | tf_op | source)
XLA Modules:
  0.0 87.2 jit_solution(15763195627312388069)
XLA Ops:
  0.6 83.9 %shard_map.41 = (f32[128,1024]{1,0:T(8,128)}, bf16[2,2,128,512]{3,2,1,0:T(8,128)(2,1)}, f32[1,1]{1,0:T(1,128)}) custom-call(bf16[128,1024]{1,0:T(8,128)(2,1)} %emb.1, s32[1,128]{1,0:T(1,128)} %bitcast.2), custom_call_target="tpu_custom_call" | custom-call | tf_op jit(solution)/shard_map/pallas_call | solution.py:651
  84.6 2.6 %shard_map.42 = (f32[128,1024]{1,0:T(8,128)}, f32[1,1]{1,0:T(1,128)}) custom-call(f32[128,1024]{1,0:T(8,128)} %get-tuple-element.7.own, bf16[2,2,128,512]{3,2,1,0:T(8,128)(2,1)} %get-tuple-element.8.parts, f32[1,1]{1,0:T(1,128)} %get-tuple-element.9.total), custom_call_target="tpu_custom_call" | custom-call | tf_op jit(solution)/shard_map/pallas_call | solution.py:706

commit v7 on v6

--- a/solution.py
+++ b/solution.py
@@ -293,11 +293,17 @@
         out = [jnp.sum(ref[pl.ds(g * BLOCK, BLOCK), :].T, axis=0, keepdims=True) for g in range(LINE)]
         return jnp.concatenate(out, axis=0)
 
+    plane_ids = [dev_of(dy, dz, 0, core) for dy, dz in FAR_FIRST]
+    line_ids = [
+        dev_of(0, 0, dx, 1 - core if other else core)
+        for dx, other in ((2, 1), (2, 0), (1, 1), (-1, 1), (1, 0), (-1, 0), (0, 1))
+    ]
+
     def send_cols(e):
-        for dy, dz in FAR_FIRST:
+        for device in plane_ids:
             pltpu.make_async_remote_copy(
                 src_ref=cmsg.at[e], dst_ref=crx.at[e, a], send_sem=csend.at[e], recv_sem=crecv.at[e],
-                device_id=(dev_of(dy, dz, 0, core),), device_id_type=MESH,
+                device_id=(device,), device_id_type=MESH,
             ).start()
         crx[e, a] = cmsg[e]
 
@@ -305,11 +311,11 @@
         return pl.ds(0, LINE + 8 if e in (0, 3) else LINE)
 
     def send_rows(e):
-        for dx, other in ((2, 1), (2, 0), (1, 1), (-1, 1), (1, 0), (-1, 0), (0, 1)):
+        for device in line_ids:
             pltpu.make_async_remote_copy(
                 src_ref=rmsg.at[e, row_part(e)], dst_ref=rrx.at[e, b, row_part(e)],
                 send_sem=rsend.at[e], recv_sem=rrecv.at[e],
-                device_id=(dev_of(0, 0, dx, 1 - core if other else core),), device_id_type=MESH,
+                device_id=(device,), device_id_type=MESH,
             ).start()
         rrx[e, b] = rmsg[e]
 
@@ -322,10 +328,10 @@
         pltpu.make_async_copy(every, every, rrecv.at[e]).wait()
 
     def send_loss():
-        for dy, dz in FAR_FIRST:
+        for device in plane_ids:
             pltpu.make_async_remote_copy(
                 src_ref=lmsg, dst_ref=lrx.at[a], send_sem=losem.at[0], recv_sem=losem.at[1],
-                device_id=(dev_of(dy, dz, 0, core),), device_id_type=MESH,
+                device_id=(device,), device_id_type=MESH,
             ).start()
         lrx[a] = lmsg[...]
 
@@ -488,13 +494,12 @@
 
         lax.fori_loop(0, steps, step, 0)
 
-    def add_first_term():
+    def keep_first_term():
         def step(i, carry):
             rows = rows_at(i)
             lr = rvec[2, rows, :]
-            qr = rvec[6, rows, :]
             for k in range(PLANE):
-                w[rows, lanes(k)] = w[rows, lanes(k)] + jnp.exp2(s[rows, lanes(k)] - lr) * qr
+                s[rows, lanes(k)] = jnp.exp2(s[rows, lanes(k)] - lr)
             return carry
 
         lax.fori_loop(0, steps, step, 0)
@@ -502,8 +507,9 @@
     def round_weights(start, count):
         def step(i, carry):
             rows = rows_at(start + i)
+            qr = rvec[6, rows, :]
             for k in range(PLANE):
-                total = w[rows, lanes(k)] + kept[rows, lanes(k)] * cvec[6, k : k + 1, :]
+                total = w[rows, lanes(k)] + kept[rows, lanes(k)] * cvec[6, k : k + 1, :] + s[rows, lanes(k)] * qr
                 wb[rows, lanes(k)] = total.astype(BF16)
             return carry
 
@@ -539,29 +545,24 @@
     lmsg[...] = jnp.sum(rrx[3, :, LINE : LINE + 8, :], axis=0)
     send_loss()
     keep_mirror(1)
+    keep_first_term()
     wait_rows(4)
     cot_r = 0.5 * cot_r + jnp.sum(rrx[4, :, 0:LINE, :], axis=0)
     to_rows(-0.5 * cot_r, rvec.at[6])
-    add_first_term()
     wait_cols(4)
     cot_c = 0.5 * cot_c + jnp.sum(crx[4], axis=0)
     cvec[6] = -0.5 * cot_c
 
     grad_scale = 1.0 / math.sqrt(WIDTH)
 
-    def product(d):
-        xx = lax.rem(x + d, SIDE)
-        round_weights(xx * (2 * BLOCK // CH), 2 * BLOCK // CH)
-        rows = pl.ds(pl.multiple_of(xx * 2 * BLOCK, 2 * BLOCK), 2 * BLOCK)
-        left = wb[rows, :]
+    def product(d, half_of):
+        block = lax.rem(x + d, SIDE) * 2 + half_of
+        round_weights(block * (BLOCK // CH), BLOCK // CH)
+        left = wb[pl.ds(pl.multiple_of(block * BLOCK, BLOCK), BLOCK), :]
         for n in range(WIDTH // TILE):
             right = ec[:, :, pl.ds(n * TILE, TILE)].reshape(CCOLS, TILE)
             out = jnp.dot(left, right, preferred_element_type=F32) * grad_scale
-            gp[d, :, :, n * TILE : (n + 1) * TILE] = out.reshape(2, BLOCK, TILE)
-        pltpu.make_async_remote_copy(
-            src_ref=gp.at[d, 1 - core], dst_ref=rb.at[d], send_sem=gsend.at[d], recv_sem=grecv.at[d],
-            device_id=(sibling,), device_id_type=MESH,
-        ).start()
+            gp[d, half_of, :, n * TILE : (n + 1) * TILE] = out
 
     def chip_sum(d):
         pltpu.make_async_copy(rb.at[d], rb.at[d], grecv.at[d]).wait()
@@ -578,9 +579,18 @@
     far, direct, near = [[ring(n, i, dx) for i, dx in ((0, 1), (1, -1))] for n in range(3)]
 
     def product_step(i, carry):
-        product(jnp.where(i == 0, 2, jnp.where(i == 1, 1, jnp.where(i == 2, 3, 0))))
-
-        @pl.when(i == 1)
+        step = i // 2
+        d = jnp.where(step == 0, 2, jnp.where(step == 1, 1, jnp.where(step == 2, 3, 0)))
+        product(d, lax.rem(i + 1 + core, 2))
+
+        @pl.when(lax.rem(i, 2) == 0)
+        def _():
+            pltpu.make_async_remote_copy(
+                src_ref=gp.at[d, 1 - core], dst_ref=rb.at[d], send_sem=gsend.at[d], recv_sem=grecv.at[d],
+                device_id=(sibling,), device_id_type=MESH,
+            ).start()
+
+        @pl.when(i == 2)
         def _():
             v = chip_sum(2).astype(BF16)
             xs[0, 0] = v[:, :half]
@@ -588,14 +598,14 @@
             xs[0, 1] = v[:, half:]
             far[1].start()
 
-        @pl.when(i == 2)
+        @pl.when(i == 4)
         def _():
             v = chip_sum(1)
             xs[1, 0] = v[:, half:].astype(BF16)
             direct[0].start()
             rb[1, :, :half] = v[:, :half]
 
-        @pl.when(i == 3)
+        @pl.when(i == 6)
         def _():
             v = chip_sum(3)
             xs[1, 1] = v[:, :half].astype(BF16)
@@ -604,7 +614,7 @@
 
         return carry
 
-    lax.fori_loop(0, SIDE, product_step, 0)
+    lax.fori_loop(0, 2 * SIDE, product_step, 0)
     far[0].wait_recv()
     xs[2, 0] = (rb[1, :, :half] + xr[0].astype(F32)).astype(BF16)
     near[0].start()

time: 87.3 us -> 86.7 us (level)
  no operation moved by 1% of the time
where the time goes in v7:
time: 86.7 us; the launch traced here: 86.5 us
  Pallas kernels  85.9 us (99%)
    pallas_call x1, Pallas kernels, shards(): pl.pallas_call(kernel, out_shape=(jax.ShapeDtypeStruct((BLOCK, WIDTH), F3...  83.3 us
    pallas_call x1, Pallas kernels, shards(): pl.pallas_call(add_parts, out_shape=(jax.ShapeDtypeStruct((BLOCK, WIDTH),...  2.58 us

profile of v7, /device:TPU:1, one launch (start us, length us, event | category | flops | bytes accessed | tf_op | source)
XLA Modules:
  0.0 86.5 jit_solution(7002307782820301609)
XLA Ops:
  0.6 83.3 %shard_map.41 = (f32[128,1024]{1,0:T(8,128)}, bf16[2,2,128,512]{3,2,1,0:T(8,128)(2,1)}, f32[1,1]{1,0:T(1,128)}) custom-call(bf16[128,1024]{1,0:T(8,128)(2,1)} %emb.1, s32[1,128]{1,0:T(1,128)} %bitcast.2), custom_call_target="tpu_custom_call" | custom-call | tf_op jit(solution)/shard_map/pallas_call | solution.py:661
  84.0 2.6 %shard_map.42 = (f32[128,1024]{1,0:T(8,128)}, f32[1,1]{1,0:T(1,128)}) custom-call(f32[128,1024]{1,0:T(8,128)} %get-tuple-element.7.own, bf16[2,2,128,512]{3,2,1,0:T(8,128)(2,1)} %get-tuple-element.8.parts, f32[1,1]{1,0:T(1,128)} %get-tuple-element.9.total), custom_call_target="tpu_custom_call" | custom-call | tf_op jit(solution)/shard_map/pallas_call | solution.py:716

commit v8 on v7

--- a/solution.py
+++ b/solution.py
@@ -171,8 +171,8 @@
     send_line(1, 0, 128, sibling, 6)
     sent(2)
     issue(4)
+    issue(5)
     sent(3)
-    issue(5)
     arrived(2)
     wait_line(xblk(2), 0, 64, 2)
     wait_line(xblk(2), 64, 64, 3)
@@ -624,10 +624,6 @@
     rb[0] = chip_sum(0)
     result = pltpu.make_async_copy(rb.at[0], own, lsem.at[2])
     result.start()
-    for c in direct + near:
-        c.wait_recv()
-    result.wait()
-
     every = lrx.at[pl.ds(0, PLANE - 1)]
     pltpu.make_async_copy(every, every, losem.at[1]).wait()
     loss[0, 0] = jnp.sum(lrx[...]) * (-LN2 / TOTAL)
@@ -644,8 +640,11 @@
         pltpu.make_async_copy(every, every, csend.at[e]).wait()
     for d in range(SIDE):
         pltpu.make_async_copy(rb.at[d], rb.at[d], gsend.at[d]).wait()
-    for c in far + direct + near:
+    for c in far:
         c.wait_send()
+    result.wait()
+    for c in direct + near:
+        c.wait()
 
 
 def add_parts(own, parts, total, grad, loss):

time: 86.7 us -> 86.5 us (level)
  no operation moved by 1% of the time
where the time goes in v8:
time: 86.5 us; the launch traced here: 86.4 us
  Pallas kernels  85.7 us (99%)
    pallas_call x1, Pallas kernels, shards(): pl.pallas_call(kernel, out_shape=(jax.ShapeDtypeStruct((BLOCK, WIDTH), F3...  83.2 us
    pallas_call x1, Pallas kernels, shards(): pl.pallas_call(add_parts, out_shape=(jax.ShapeDtypeStruct((BLOCK, WIDTH),...  2.58 us

profile of v8, /device:TPU:1, one launch (start us, length us, event | category | flops | bytes accessed | tf_op | source)
XLA Modules:
  0.0 86.4 jit_solution(7797413467412790252)
XLA Ops:
  0.6 83.2 %shard_map.41 = (f32[128,1024]{1,0:T(8,128)}, bf16[2,2,128,512]{3,2,1,0:T(8,128)(2,1)}, f32[1,1]{1,0:T(1,128)}) custom-call(bf16[128,1024]{1,0:T(8,128)(2,1)} %emb.1, s32[1,128]{1,0:T(1,128)} %bitcast.2), custom_call_target="tpu_custom_call" | custom-call | tf_op jit(solution)/shard_map/pallas_call | solution.py:660
  83.8 2.6 %shard_map.42 = (f32[128,1024]{1,0:T(8,128)}, f32[1,1]{1,0:T(1,128)}) custom-call(f32[128,1024]{1,0:T(8,128)} %get-tuple-element.7.own, bf16[2,2,128,512]{3,2,1,0:T(8,128)(2,1)} %get-tuple-element.8.parts, f32[1,1]{1,0:T(1,128)} %get-tuple-element.9.total), custom_call_target="tpu_custom_call" | custom-call | tf_op jit(solution)/shard_map/pallas_call | solution.py:715
